TPU v7x, 512 devices: a whole 4x4x16 slice. The times are simulated.
512 devices in a mesh: branch: 8 (over z_lo), tok: 64 (over y, z_hi, x, core).
Axes of the slice: x: 4, y: 4, z: 16 (z_hi: 2, z_lo: 8; z = z_hi * 8 + z_lo), core: 2. Of those that a mesh axis runs over, the one named last changes fastest.
Arguments:
- teacher_hidden: bfloat16 [8, 1024, 4096], P('branch', 'tok'), may hold values from -400 to 400
- teacher_gain: float32 [8, 4096], P('branch'), may hold values from 0.5 to 1.5
- teacher_head: bfloat16 [8, 4096, 20480], P('branch', None, 'tok'), may hold values from -30 to 30
- student_hidden: bfloat16 [1024, 4096], P('branch'), may hold values from -400 to 400
- student_gain: float32 [4096], replicated, may hold values from 0.5 to 1.5
- student_head: bfloat16 [4096, 20480], P('branch', 'tok'), may hold values from -30 to 30
- cluster_weights: int32 [1024, 8], P(None, 'branch'), may hold values from 0 to 64, as said below
- token_ids: int32 [1024], P('branch'), may hold values from 0 to 20479
Outputs:
- grad_head: float32 [4096, 20480], P('branch', 'tok')
- grad_hidden: float32 [1024, 4096], P('branch', 'tok')
- grad_gain: float32 [4096], P('tok')
Inputs may be any that keep to these rules, and one draw needn't show every extreme that they name: `cluster_weights`: each token's 8 weights sum to 64.
All inputs are finite; a program needn't handle non-finite values.
Results may differ from a plain program's by a relative error of at most 0.0063.
Values may be sent and summed in bfloat16 or wider, within the bound.
A program may use at most 64 MiB of HBM per device.

v0:
```python
import jax
import jax.numpy as jnp
from jax import lax
from jax.sharding import Mesh
from jax.sharding import PartitionSpec as P

DEN = 64
TOK = ("tok_0", "tok_1", "tok_2", "tok_3")


eps = 1e-05
mix_label = 0.25
loss_scale = 64.0


def copy_for_each(value, axis):
    copies = jnp.broadcast_to(value, (lax.axis_size(axis), *value.shape))
    return lax.all_to_all(copies, axis, split_axis=0, concat_axis=0, tiled=True)


def collected_together(value, axis):
    leaves = jax.tree.leaves(value)
    turns = sorted(range(len(leaves)), key=lambda k: -leaves[k].size)
    width = (1, *leaves[turns[0]].shape)[-1]
    lines = [
        jnp.pad(leaves[k].reshape(-1), (0, -leaves[k].size % width)).reshape(-1, width)
        for k in turns
    ]
    both, at, found = (copy_for_each(jnp.concatenate(lines), axis), 0, {})
    for k, line in zip(turns, lines):
        slab = both[:, at : at + len(line)].reshape(len(both), -1)
        found[k] = slab[:, : leaves[k].size].reshape(-1, *leaves[k].shape)
        at += len(line)
    numbers = iter(range(len(leaves)))
    return jax.tree.map(lambda _: found[next(numbers)], value)


def joined_by_halves(pieces, combine):
    while len(jax.tree.leaves(pieces)[0]) > 1:
        pieces = jax.vmap(combine)(
            *(jax.tree.map(lambda part: part[side::2], pieces) for side in (0, 1))
        )
    return jax.tree.map(lambda part: part[0], pieces)


def joined_all(value, axis, combine):
    pieces = collected_together(value, axis)
    return joined_by_halves(pieces, combine)


def cut_along(value, dim, size):
    dims = value.shape
    blocks = value.reshape(*dims[:dim], size, dims[dim] // size, *dims[dim + 1 :])
    return jnp.moveaxis(blocks, dim, 0)


def summed_on_arrival(value, axis, dim):
    blocks = cut_along(value, dim, lax.axis_size(axis))
    arrived = lax.all_to_all(blocks, axis, split_axis=0, concat_axis=0, tiled=True)
    return arrived.sum(axis=0)


def in_order(blocks, dim):
    dims = list(blocks.shape[1:])
    dims[dim] *= blocks.shape[0]
    return jnp.moveaxis(blocks, 0, dim).reshape(dims)


def gathered_copies(value, axis, dim):
    blocks = copy_for_each(value, axis)
    return in_order(blocks, dim)


def summed_rows(value, axes, dim):
    far, near = axes
    blocks = cut_along(value, dim, lax.axis_size(far))
    nearer = summed_on_arrival(blocks, near, dim + 1)
    arrived = lax.all_to_all(nearer, far, split_axis=0, concat_axis=0, tiled=True)
    return arrived.sum(axis=0)


def over_copies(value, axis):
    everything = copy_for_each(value, axis)
    return jnp.sum(everything, axis=0)


def normalize(hidden, gain):
    values = hidden.astype(jnp.float32)
    inv_scale = lax.rsqrt(jnp.mean(values * values, axis=-1, keepdims=True) + eps)
    return ((values * inv_scale * gain).astype(jnp.bfloat16), inv_scale)


def combine_stats(first, second):
    top = jnp.maximum(first[0], second[0])
    return (top, first[1] * jnp.exp(first[0] - top) + second[1] * jnp.exp(second[0] - top))


def probabilities(logits):
    local_max = jnp.max(logits, axis=1)
    local_scaled = jnp.exp(logits - local_max[:, None])
    row_max, row_total = joined_all((local_max, jnp.sum(local_scaled, axis=1)), TOK, combine_stats)
    scaled = local_scaled * jnp.exp(local_max - row_max)[:, None]
    return scaled / row_total[:, None]


def per_device(
    teacher_hidden,
    teacher_gain,
    teacher_head,
    student_hidden,
    student_gain,
    student_head,
    cluster_weights,
    token_ids,
):
    width = student_hidden.shape[1]
    head_cols = teacher_head.shape[2]
    branch_gain = teacher_gain[0]
    branch_head = teacher_head[0]
    normed, unused_scale = normalize(
        lax.all_gather(teacher_hidden[0], TOK, axis=0, tiled=True), branch_gain
    )
    teacher_logits = jnp.dot(normed, branch_head, preferred_element_type=jnp.float32)
    weight = cluster_weights[:, 0].astype(jnp.float32) / DEN
    terms = probabilities(teacher_logits) * weight[:, None]
    mixed = summed_on_arrival(terms, "branch", 0)
    student_normed, inv_scale = normalize(student_hidden, student_gain)
    whole_head = gathered_copies(student_head, "branch", 0)
    student_logits = jnp.dot(student_normed, whole_head, preferred_element_type=jnp.float32)
    student_probs = probabilities(student_logits)
    offset = lax.axis_index(TOK) * head_cols
    onehot = (
        token_ids[:, None] == offset + jnp.arange(head_cols, dtype=jnp.int32)[None, :]
    ).astype(jnp.float32)
    targets = (1.0 - mix_label) * mixed + mix_label * onehot
    logit_grads = (loss_scale * (student_probs - targets)).astype(jnp.bfloat16)
    contract = (((1,), (1,)), ((), ()))
    partial_grads = lax.dot_general(
        logit_grads, whole_head, contract, preferred_element_type=jnp.float32
    )
    normed_grads = summed_rows(partial_grads, (("tok_0", "tok_1", "tok_2"), "tok_3"), 1)
    slice_width = normed_grads.shape[1]
    col_start = lax.axis_index(TOK) * slice_width
    hidden_cols = lax.dynamic_slice_in_dim(student_hidden, col_start, slice_width, 1).astype(
        jnp.float32
    )
    gain_cols = lax.dynamic_slice_in_dim(student_gain, col_start, slice_width, 0)
    grad_gain = over_copies(jnp.sum(normed_grads * hidden_cols * inv_scale, axis=0), "branch")
    row_dots = over_copies(jnp.sum(gain_cols[None, :] * normed_grads * hidden_cols, axis=1), TOK)
    grad_hidden = (
        inv_scale * gain_cols[None, :] * normed_grads
        - hidden_cols * inv_scale**3 * row_dots[:, None] / width
    )
    exchanged = lax.all_to_all(student_normed, "branch", split_axis=1, concat_axis=0, tiled=True)
    all_grads = gathered_copies(logit_grads, "branch", 0)
    grad_head = lax.dot_general(
        exchanged, all_grads, (((0,), (0,)), ((), ())), preferred_element_type=jnp.float32
    )
    return (grad_head, grad_hidden, grad_gain)


def solution(mesh):
    split = Mesh(
        mesh.devices.reshape(mesh.shape["branch"], 4, 2, 4, 2),
        ("branch", "tok_0", "tok_1", "tok_2", "tok_3"),
    )
    in_specs = (
        P("branch", TOK, None),
        P("branch", None),
        P("branch", None, TOK),
        P("branch", None),
        P(),
        P("branch", TOK),
        P(None, "branch"),
        P("branch"),
    )
    out_specs = (P("branch", TOK), P("branch", TOK), P(TOK))
    return jax.shard_map(
        per_device, mesh=split, in_specs=in_specs, out_specs=out_specs, check_vma=False
    )
```

profile of v0, /device:TPU:1, one launch (start us, length us, event | category | flops | bytes accessed | tf_op | source)
XLA Modules:
  0.0 602.1 jit_solution(17609629686330054629)
XLA Ops:
  7.2 0.7 all-gather.3.cloned.1.call-update
  7.9 2.8 broadcast_in_dim.12
  10.7 13.1 %all-to-all-start.1 = ((bf16[8,512,320]{1,2,0:T(8,128)(2,1)}), bf16[8,512,320]{1,2,0:T(8,128)(2,1)}, u32[]{:S(2)}, u32[]{:S(2)}) async-start(bf16[8,512,320]{1,2,0:T(8,128)(2,1)} %broadcast_in_dim.12), calls=%async_computation.1 | async-start | bytes 5242880 | tf_op jit(solution)/shard_map/all_to_all | solution.py:18
  23.8 2.3 copy.51
  26.1 210.6 %all-gather.3.cloned.1.call-done = bf16[1,1024,4096]{2,1,0:T(8,128)(2,1)} async-done(((bf16[1,16,4096]{2,1,0:T(8,128)(2,1)}), bf16[1,1024,4096]{2,1,0:T(8,128)(2,1)}) %all-gather.3.cloned.1.call-update) | async-done | bytes 8388624 | tf_op jit(solution)/shard_map/all_gather | solution.py:121
  236.7 5.2 fusion
  242.0 0.5 copy-done.2
  242.5 3.3 fusion.28
  245.8 1.0 copy-done.3
  247.0 0.9 broadcast_in_dim.14
  248.0 6.0 all-to-all-start.3
  253.9 1.8 fusion.11
  255.7 1.7 fusion.13
  257.5 2.4 copy.69
  259.9 0.9 fusion.29
  260.9 26.4 %all-to-all-done.3 = f32[64,2,1024]{2,1,0:T(2,128)S(1)} async-done(((f32[64,2,1024]{2,1,0:T(2,128)}), f32[64,2,1024]{2,1,0:T(2,128)S(1)}, u32[]{:S(2)}, u32[]{:S(2)}) %all-to-all-start.3) | async-done | bytes 524320 | tf_op jit(solution)/shard_map/all_to_all | solution.py:18
  287.3 0.6 broadcast_in_dim.13
  288.0 7.5 %all-to-all-start.2 = ((f32[64,2,128]{2,1,0:T(2,128)}), f32[64,2,128]{2,1,0:T(2,128)S(1)}, u32[]{:S(2)}, u32[]{:S(2)}) async-start(f32[64,2,128]{2,1,0:T(2,128)} %broadcast_in_dim.13), calls=%async_computation.2 | async-start | bytes 131072 | tf_op jit(solution)/shard_map/all_to_all | solution.py:18
  295.5 0.4 fusion.26
  296.1 0.7 slice.204
  296.8 1.0 multiply_add_fusion
  298.4 2.7 copy_bitcast_fusion.1
  301.1 11.2 %all-to-all-done.2 = f32[64,2,128]{2,1,0:T(2,128)S(1)} async-done(((f32[64,2,128]{2,1,0:T(2,128)}), f32[64,2,128]{2,1,0:T(2,128)S(1)}, u32[]{:S(2)}, u32[]{:S(2)}) %all-to-all-start.2) | async-done | bytes 65568 | tf_op jit(solution)/shard_map/all_to_all | solution.py:18
  312.3 13.7 %all-to-all-start.4 = ((f32[8,128,320]{1,2,0:T(8,128)}), f32[8,128,320]{1,2,0:T(8,128)}, u32[]{:S(2)}, u32[]{:S(2)}) async-start(f32[8,128,320]{1,2,0:T(8,128)} %copy_bitcast_fusion.1), calls=%async_computation.4 | async-start | bytes 2621440 | tf_op jit(solution)/shard_map/all_to_all | solution.py:59
  326.0 2.3 copy.52
  328.2 4.7 copy.53
  332.9 5.3 dot_general.17
  338.8 49.2 %all-to-all-done.4 = f32[8,128,320]{1,2,0:T(8,128)} async-done(((f32[8,128,320]{1,2,0:T(8,128)}), f32[8,128,320]{1,2,0:T(8,128)}, u32[]{:S(2)}, u32[]{:S(2)}) %all-to-all-start.4) | async-done | bytes 1310752 | tf_op jit(solution)/shard_map/all_to_all | solution.py:59
  387.9 1.4 reduce_sum.103
  389.5 3.2 fusion.9
  392.7 0.2 copy.76
  392.9 7.5 %all_to_all.63 = f32[2,32,128,64]{2,3,1,0:T(8,128)} all-to-all(f32[2,32,128,64]{2,3,1,0:T(8,128)S(1)} %bitcast.68), channel_id=1, replica_groups=mesh['branch'=8,'tok_0'=4,'tok_1'=2,'tok_2'=4,'tok_3'=2] {'tok_3'}, dimensions={0} | all-to-all | bytes 4194304 | tf_op jit(solution)/shard_map/all_to_all | solution.py:59
  400.4 4.2 all-to-all-start
  404.7 2.8 reduce_sum.104
  407.5 48.0 %all-to-all-done = bf16[128,8,512]{2,0,1:T(8,128)(2,1)} async-done(((bf16[128,8,512]{2,0,1:T(8,128)(2,1)}), bf16[128,8,512]{2,0,1:T(8,128)(2,1)}, u32[]{:S(2)}, u32[]{:S(2)}) %all-to-all-start) | async-done | bytes 1048608 | tf_op jit(solution)/shard_map/all_to_all | solution.py:154
  455.5 51.6 %all_to_all.64 = f32[32,128,64]{1,2,0:T(8,128)} all-to-all(f32[32,128,64]{1,2,0:T(8,128)} %reduce_sum.104), channel_id=1, replica_groups=mesh['branch'=8,'tok_0'=4,'tok_1'=2,'tok_2'=4,'tok_3'=2] {'tok_0','tok_1..., dimensions={0} | all-to-all | bytes 2097152 | tf_op jit(solution)/shard_map/all_to_all | solution.py:78
  507.0 0.9 broadcast_in_dim.15
  507.9 14.0 %all-to-all-start.5 = ((bf16[8,128,320]{1,2,0:T(8,128)(2,1)}), bf16[8,128,320]{1,2,0:T(8,128)(2,1)S(1)}, u32[]{:S(2)}, u32[]{:S(2)}) async-start(bf16[8,128,320]{1,2,0:T(8,128)(2,1)} %broadcast_in_dim.15), calls=%async_computation.5 | async-start | bytes 1310720 | tf_op jit(solution)/shard_map/all_to_all | solution.py:18
  522.0 1.3 reduce_sum.105
  523.3 0.9 fusion.23
  524.2 21.7 %all-to-all-done.5 = bf16[8,128,320]{1,2,0:T(8,128)(2,1)S(1)} async-done(((bf16[8,128,320]{1,2,0:T(8,128)(2,1)}), bf16[8,128,320]{1,2,0:T(8,128)(2,1)S(1)}, u32[]{:S(2)}, u32[]{:S(2)}) %all-to-all-start.5) | async-done | bytes 655392 | tf_op jit(solution)/shard_map/all_to_all | solution.py:18
  546.0 22.7 %all_to_all.65 = f32[8,1,64]{2,1,0:T(1,128)S(1)} all-to-all(f32[8,1,64]{2,1,0:T(1,128)S(1)} %broadcast_in_dim.17), channel_id=1, replica_groups=mesh['branch'=8,'tok_0'=4,'tok_1'=2,'tok_2'=4,'tok_3'=2] {'branch'}, dimensions={0} | all-to-all | bytes 4096 | tf_op jit(solution)/shard_map/all_to_all | solution.py:18
  568.6 0.6 broadcast_in_dim.16
  569.3 8.1 %all-to-all-start.8 = ((f32[64,1,128]{2,1,0:T(1,128)}), f32[64,1,128]{2,1,0:T(1,128)S(1)}, u32[]{:S(2)}, u32[]{:S(2)}) async-start(f32[64,1,128]{2,1,0:T(1,128)} %broadcast_in_dim.16), calls=%async_computation.8 | async-start | bytes 65536 | tf_op jit(solution)/shard_map/all_to_all | solution.py:18
  577.4 2.6 convolution_bitcast_fusion
  580.0 0.5 reduce_sum.109
  580.5 13.3 %all-to-all-done.8 = f32[64,1,128]{2,1,0:T(1,128)S(1)} async-done(((f32[64,1,128]{2,1,0:T(1,128)}), f32[64,1,128]{2,1,0:T(1,128)S(1)}, u32[]{:S(2)}, u32[]{:S(2)}) %all-to-all-start.8) | async-done | bytes 32800 | tf_op jit(solution)/shard_map/all_to_all | solution.py:18
  593.8 1.4 fusion.20
  (82 shorter events, 1.8 us)
Async XLA Ops:
  7.2 234.8 %copy-start = (bf16[1,4096,320]{1,2,0:T(8,128)(2,1)S(1)}, bf16[1,4096,320]{1,2,0:T(8,128)(2,1)}, u32[]{:S(2)}) copy-start(bf16[1,4096,320]{1,2,0:T(8,128)(2,1)} %param.10) | copy-start | bytes 7864324
  7.2 229.5 %all-gather.3.cloned.1.call-start = ((), (), s32[]{:S(2)}) async-start(), calls=%async_computation.10 | async-start | bytes 8519680 | tf_op jit(solution)/shard_map/all_gather | solution.py:121
  10.7 236.3 %all-to-all-start.1 = ((bf16[8,512,320]{1,2,0:T(8,128)(2,1)}), bf16[8,512,320]{1,2,0:T(8,128)(2,1)}, u32[]{:S(2)}, u32[]{:S(2)}) async-start(bf16[8,512,320]{1,2,0:T(8,128)(2,1)} %broadcast_in_dim.12), calls=%async_computation.1 | async-start | bytes 5242880 | tf_op jit(solution)/shard_map/all_to_all | solution.py:18
  23.8 218.1 %copy-start.7 = (f32[1,4096]{1,0:T(1,128)S(1)}, f32[1,4096]{1,0:T(1,128)}, u32[]{:S(2)}) copy-start(f32[1,4096]{1,0:T(1,128)} %param.9) | copy-start | bytes 49156
  236.7 5.8 copy-start.2
  245.7 1.0 copy-start.3
  245.8 10.0 %copy-start.5 = (s32[1024,1]{0,1:T(1,128)S(1)}, s32[1024,1]{0,1:T(1,128)}, u32[]{:S(2)}) copy-start(s32[1024,1]{0,1:T(1,128)} %param.14) | copy-start | bytes 12292
  245.8 10.0 %copy-start.4 = (f32[4096]{0:T(1024)S(1)}, f32[4096]{0:T(1024)}, u32[]{:S(2)}) copy-start(f32[4096]{0:T(1024)} %param.12) | copy-start | bytes 49156
  248.0 39.4 %all-to-all-start.3 = ((f32[64,2,1024]{2,1,0:T(2,128)}), f32[64,2,1024]{2,1,0:T(2,128)S(1)}, u32[]{:S(2)}, u32[]{:S(2)}) async-start(f32[64,2,1024]{2,1,0:T(2,128)} %broadcast_in_dim.14), calls=%async_computation.3 | async-start | bytes 1048576 | tf_op jit(solution)/shard_map/all_to_all | solution.py:18
  257.5 2.4 copy-start.1
  288.0 24.3 %all-to-all-start.2 = ((f32[64,2,128]{2,1,0:T(2,128)}), f32[64,2,128]{2,1,0:T(2,128)S(1)}, u32[]{:S(2)}, u32[]{:S(2)}) async-start(f32[64,2,128]{2,1,0:T(2,128)} %broadcast_in_dim.13), calls=%async_computation.2 | async-start | bytes 131072 | tf_op jit(solution)/shard_map/all_to_all | solution.py:18
  312.3 75.7 %all-to-all-start.4 = ((f32[8,128,320]{1,2,0:T(8,128)}), f32[8,128,320]{1,2,0:T(8,128)}, u32[]{:S(2)}, u32[]{:S(2)}) async-start(f32[8,128,320]{1,2,0:T(8,128)} %copy_bitcast_fusion.1), calls=%async_computation.4 | async-start | bytes 2621440 | tf_op jit(solution)/shard_map/all_to_all | solution.py:59
  332.9 56.4 %copy-start.6 = (s32[128]{0:T(128)S(1)}, s32[128]{0:T(128)}, u32[]{:S(2)}) copy-start(s32[128]{0:T(128)} %param.15) | copy-start | bytes 1540
  400.4 55.1 %all-to-all-start = ((bf16[128,8,512]{2,0,1:T(8,128)(2,1)}), bf16[128,8,512]{2,0,1:T(8,128)(2,1)}, u32[]{:S(2)}, u32[]{:S(2)}) async-start(bf16[128,8,512]{2,0,1:T(8,128)(2,1)} %copy.52), calls=%async_computation | async-start | bytes 2097152 | tf_op jit(solution)/shard_map/all_to_all | solution.py:154
  507.9 38.0 %all-to-all-start.5 = ((bf16[8,128,320]{1,2,0:T(8,128)(2,1)}), bf16[8,128,320]{1,2,0:T(8,128)(2,1)S(1)}, u32[]{:S(2)}, u32[]{:S(2)}) async-start(bf16[8,128,320]{1,2,0:T(8,128)(2,1)} %broadcast_in_dim.15), calls=%async_computation.5 | async-start | bytes 1310720 | tf_op jit(solution)/shard_map/all_to_all | solution.py:18
  569.3 24.6 %all-to-all-start.8 = ((f32[64,1,128]{2,1,0:T(1,128)}), f32[64,1,128]{2,1,0:T(1,128)S(1)}, u32[]{:S(2)}, u32[]{:S(2)}) async-start(f32[64,1,128]{2,1,0:T(1,128)} %broadcast_in_dim.16), calls=%async_computation.8 | async-start | bytes 65536 | tf_op jit(solution)/shard_map/all_to_all | solution.py:18
Sparse Core Ops, SparseCore 0:
  12.6 224.0 all-gather.2
where the time goes:
time: 603 us; the launch traced here: 602 us
  waiting for transfers between devices  381 us (63%)
  blocking collectives  81.7 us (14%)
  starting transfers between devices  66.6 us (11%)
  local copies, waits for them, and re-layouts  26.8 us (4%)
  other arithmetic  21.5 us (4%)
  between operations  14.4 us (2%)
  matrix products  9.89 us (2%)
    all_gather x1, waiting for transfers between devices, per_device(): lax.all_gather(teacher_hidden[0], TOK, axis=0, tiled=True)  211 us
    all_to_all x5, waiting for transfers between devices, copy_for_each(): return lax.all_to_all(copies, axis, split_axis=0, concat_axis=0, tiled=True)  72.7 us
    all_to_all x1, blocking collectives, summed_rows(): lax.all_to_all(nearer, far, split_axis=0, concat_axis=0, tiled=True)  51.6 us
    all_to_all x1, waiting for transfers between devices, summed_on_arrival(): lax.all_to_all(blocks, axis, split_axis=0, concat_axis=0, tiled=True)  49.2 us
    all_to_all x5, starting transfers between devices, copy_for_each(): return lax.all_to_all(copies, axis, split_axis=0, concat_axis=0, tiled=True)  48.7 us
    all_to_all x1, waiting for transfers between devices, per_device(): lax.all_to_all(student_normed, 'branch', split_axis=1, concat_axis=0, til...  48 us
    all_to_all x1, blocking collectives, copy_for_each(): return lax.all_to_all(copies, axis, split_axis=0, concat_axis=0, tiled=True)  22.7 us
    all_to_all x1, starting transfers between devices, summed_on_arrival(): lax.all_to_all(blocks, axis, split_axis=0, concat_axis=0, tiled=True)  13.7 us
  transfers between devices with their start and end apart: 8, of which 7 were waited for; matrix products, arithmetic and copies ran while one was open for 8% of the time, Pallas kernels for 0%

commit v1 on v0

--- a/solution.py
+++ b/solution.py
@@ -1,11 +1,145 @@
 import jax
 import jax.numpy as jnp
 from jax import lax
+from jax.experimental import pallas as pl
+from jax.experimental.pallas import tpu as pltpu
 from jax.sharding import Mesh
 from jax.sharding import PartitionSpec as P
 
 DEN = 64
-TOK = ("tok_0", "tok_1", "tok_2", "tok_3")
+Y, H, X, C = "tok_0", "tok_1", "tok_2", "tok_3"
+TOK = (Y, H, X, C)
+MESH = pl.DeviceIdType.MESH
+
+
+def ring(value, step, size):
+    return lax.rem(value + (step + size), size)
+
+
+def gather_kernel(block_ref, out_ref, local_sem, send_sem, recv_sem):
+    y, h, x, c = (lax.axis_index(name) for name in TOK)
+    width = block_ref.shape[1]
+    half = width // 2
+    barrier = pltpu.get_barrier_semaphore()
+    peers = (
+        {X: ring(x, 1, 4)}, {X: ring(x, -1, 4)}, {Y: ring(y, 1, 4)}, {Y: ring(y, -1, 4)},
+        {H: 1 - h}, {C: 1 - c},
+    )
+    for peer in peers:
+        pl.semaphore_signal(barrier, inc=1, device_id=peer, device_id_type=MESH)
+    pl.semaphore_wait(barrier, len(peers))
+
+    numbers = iter(range(64))
+    sent = []
+
+    def move(piece, peer, arriving, first=None):
+        number = next(numbers)
+        copy = pltpu.make_async_remote_copy(
+            src_ref=piece if first is None else first, dst_ref=piece, send_sem=send_sem.at[number],
+            recv_sem=recv_sem.at[number], device_id=peer, device_id_type=MESH,
+        )
+        copy.start()
+        sent.append(copy)
+        incoming = pltpu.make_async_remote_copy(
+            src_ref=arriving, dst_ref=arriving, send_sem=send_sem.at[number],
+            recv_sem=recv_sem.at[number], device_id=peer, device_id_type=MESH,
+        )
+        return incoming.wait_recv
+
+    def blocks(ys, hs, xs, core, cols):
+        return out_ref.at[ys, hs, xs, core, :, cols]
+
+    own = pltpu.make_async_copy(block_ref, out_ref.at[y, h, x, c], local_sem)
+    own.start()
+    everything = pl.ds(0, width)
+    across = move(blocks(y, h, x, c, everything), {H: 1 - h}, blocks(y, 1 - h, x, c, everything), block_ref)
+    last = []
+
+    def route(side, plane, fresh):
+        start = side * half
+        cols = pl.ds(start, half)
+        quarters = (pl.ds(start, half // 2), pl.ds(start + half // 2, half // 2))
+        axis, other = ((X, Y), (Y, X))[side]
+        mine, theirs = ((x, y), (y, x))[side]
+
+        def near(step, cs):
+            at = ring(mine, step, 4)
+            return blocks(y, plane, at, c, cs) if side == 0 else blocks(at, plane, x, c, cs)
+
+        def rows(step, core, cs):
+            at = ring(theirs, step, 4)
+            every = pl.ds(0, 4)
+            return blocks(at, plane, every, core, cs) if side == 0 else blocks(every, plane, at, core, cs)
+
+        def to(name, step):
+            return {name: ring(mine if name == axis else theirs, step, 4)}
+
+        def share(step):
+            last.append(move(rows(step, c, cols), {C: 1 - c}, rows(step, 1 - c, cols)))
+
+        first = block_ref.at[:, cols] if fresh else None
+        up = move(near(0, cols), to(axis, 1), near(-1, cols), first)
+        down = move(near(0, cols), to(axis, -1), near(1, cols), first)
+        yield
+        up()
+        far_up = move(near(-1, quarters[0]), to(axis, 1), near(2, quarters[0]))
+        down()
+        far_down = move(near(1, quarters[1]), to(axis, -1), near(2, quarters[1]))
+        yield
+        far_up()
+        far_down()
+        up = move(rows(0, c, cols), to(other, 1), rows(-1, c, cols))
+        down = move(rows(0, c, cols), to(other, -1), rows(1, c, cols))
+        share(0)
+        yield
+        up()
+        far_up = move(rows(-1, c, quarters[0]), to(other, 1), rows(2, c, quarters[0]))
+        down()
+        far_down = move(rows(1, c, quarters[1]), to(other, -1), rows(2, c, quarters[1]))
+        share(-1)
+        share(1)
+        yield
+        far_up()
+        far_down()
+        share(2)
+
+    routes = [route(0, h, True), route(1, h, True)]
+    for turn in range(4):
+        if turn == 2:
+            own.wait()
+        for r in routes:
+            next(r)
+    across()
+    late = [route(0, 1 - h, False), route(1, 1 - h, False)]
+    for r in late:
+        next(r)
+    for r in routes:
+        next(r, None)
+    for _ in range(4):
+        for r in late:
+            next(r, None)
+    for arrive in last:
+        arrive()
+    for copy in sent:
+        copy.wait_send()
+
+
+def gather_tokens(block):
+    rows, width = block.shape
+    out = pl.pallas_call(
+        gather_kernel,
+        out_shape=jax.ShapeDtypeStruct((4, 2, 4, 2, rows, width), block.dtype),
+        in_specs=[pl.BlockSpec(memory_space=pl.ANY)],
+        out_specs=pl.BlockSpec(memory_space=pl.ANY),
+        scratch_shapes=[
+            pltpu.SemaphoreType.DMA,
+            pltpu.SemaphoreType.DMA((64,)),
+            pltpu.SemaphoreType.DMA((64,)),
+        ],
+        compiler_params=pltpu.CompilerParams(collective_id=0, has_side_effects=True),
+        name="gather_tokens",
+    )(block)
+    return out.reshape(64 * rows, width)
 
 
 eps = 1e-05
@@ -117,9 +251,8 @@
     head_cols = teacher_head.shape[2]
     branch_gain = teacher_gain[0]
     branch_head = teacher_head[0]
-    normed, unused_scale = normalize(
-        lax.all_gather(teacher_hidden[0], TOK, axis=0, tiled=True), branch_gain
-    )
+    own_normed, unused_scale = normalize(teacher_hidden[0], branch_gain)
+    normed = gather_tokens(own_normed)
     teacher_logits = jnp.dot(normed, branch_head, preferred_element_type=jnp.float32)
     weight = cluster_weights[:, 0].astype(jnp.float32) / DEN
     terms = probabilities(teacher_logits) * weight[:, None]

time: 603 us -> 543 us (0.900)
  waiting for transfers between devices: 381 us -> 253 us
  Pallas kernels: 0 us -> 58.1 us
  blocking collectives: 81.7 us -> 125 us
  starting transfers between devices: 66.6 us -> 51 us
  between operations: 14.4 us -> 1.03 us
    all_gather x1 -> x0, waiting for transfers between devices: 211 us -> none  [per_device(): lax.all_gather(teacher_hidden[0], TOK, axis=0, tiled=True)]
    all_to_all x5 -> x4, waiting for transfers between devices: 72.7 us -> 152 us  [copy_for_each(): return lax.all_to_all(copies, axis, split_axis=0, concat_axis=0, tiled=True)]
    pallas_call x0 -> x1, Pallas kernels: none -> 58.1 us  [gather_tokens(): pl.pallas_call(gather_kernel, out_shape=jax.ShapeDtypeStruct((4, 2, 4, 2,...]
    all_to_all x1 -> x2, blocking collectives: 22.7 us -> 59.6 us  [copy_for_each(): return lax.all_to_all(copies, axis, split_axis=0, concat_axis=0, tiled=True)]
    all_to_all x1, starting transfers between devices: 13.7 us -> 5.29 us  [summed_on_arrival(): lax.all_to_all(blocks, axis, split_axis=0, concat_axis=0, tiled=True)]
    all_to_all x1, blocking collectives: 51.6 us -> 59.3 us  [summed_rows(): lax.all_to_all(nearer, far, split_axis=0, concat_axis=0, tiled=True)]
    all_to_all x5 -> x4, starting transfers between devices: 48.7 us -> 41.5 us  [copy_for_each(): return lax.all_to_all(copies, axis, split_axis=0, concat_axis=0, tiled=True)]
  transfers between devices with their start and end apart: 8 -> 6, of which waited for: 7 -> 6; matrix products, arithmetic and copies ran while one was open for 8% -> 6% of each run, Pallas kernels for 0% -> 0%
where the time goes in v1:
time: 543 us; the launch traced here: 542 us
  waiting for transfers between devices  253 us (47%)
  blocking collectives  125 us (23%)
  Pallas kernels  58.1 us (11%)
  starting transfers between devices  51 us (9%)
  local copies, waits for them, and re-layouts  23.9 us (4%)
  other arithmetic  18.2 us (3%)
  matrix products  12 us (2%)
    all_to_all x4, waiting for transfers between devices, copy_for_each(): return lax.all_to_all(copies, axis, split_axis=0, concat_axis=0, tiled=True)  152 us
    all_to_all x2, blocking collectives, copy_for_each(): return lax.all_to_all(copies, axis, split_axis=0, concat_axis=0, tiled=True)  59.6 us
    all_to_all x1, blocking collectives, summed_rows(): lax.all_to_all(nearer, far, split_axis=0, concat_axis=0, tiled=True)  59.3 us
    pallas_call x1, Pallas kernels, gather_tokens(): pl.pallas_call(gather_kernel, out_shape=jax.ShapeDtypeStruct((4, 2, 4, 2,...  58.1 us
    all_to_all x1, waiting for transfers between devices, summed_on_arrival(): lax.all_to_all(blocks, axis, split_axis=0, concat_axis=0, tiled=True)  52.6 us
    all_to_all x1, waiting for transfers between devices, per_device(): lax.all_to_all(student_normed, 'branch', split_axis=1, concat_axis=0, til...  47.9 us
    all_to_all x4, starting transfers between devices, copy_for_each(): return lax.all_to_all(copies, axis, split_axis=0, concat_axis=0, tiled=True)  41.5 us
  transfers between devices with their start and end apart: 6, of which 6 were waited for; matrix products, arithmetic and copies ran while one was open for 6% of the time, Pallas kernels for 0%

profile of v1, /device:TPU:1, one launch (start us, length us, event | category | flops | bytes accessed | tf_op | source)
XLA Modules:
  0.0 542.0 jit_solution(8630681528275086352)
XLA Ops:
  0.6 1.2 fusion.9
  1.9 1.7 fusion.11.block_ref
  3.5 58.1 %gather_tokens.1 = bf16[4,2,4,2,16,4096]{5,4,3,2,1,0:T(8,128)(2,1)} custom-call(bf16[16,4096]{1,0:T(8,128)(2,1)} %fusion.11.block_ref), custom_call_target="tpu_custom_call" | custom-call | tf_op jit(solution)/shard_map/gather_tokens/pallas_call | solution.py:129
  61.6 5.3 fusion.24
  67.0 1.0 copy-done.2
  68.0 0.2 fusion.7
  68.2 0.1 broadcast_in_dim.14
  68.4 36.9 %all_to_all.63 = f32[64,2,1024]{2,1,0:T(2,128)S(1)} all-to-all(f32[64,2,1024]{2,1,0:T(2,128)S(1)} %broadcast_in_dim.14), channel_id=1, replica_groups=mesh['branch'=8,'tok_0'=4,'tok_1'=2,'tok_2'=4,'tok_3'=2] {'tok_0','tok_1..., dimensions={0} | all-to-all | bytes 1048576 | tf_op jit(solution)/shard_map/all_to_all | solution.py:152
  105.3 1.8 broadcast_in_dim.12
  107.1 13.2 %all-to-all-start.1 = ((bf16[8,512,320]{1,2,0:T(8,128)(2,1)}), bf16[8,512,320]{1,2,0:T(8,128)(2,1)}, u32[]{:S(2)}, u32[]{:S(2)}) async-start(bf16[8,512,320]{1,2,0:T(8,128)(2,1)} %broadcast_in_dim.12), calls=%async_computation.1 | async-start | bytes 5242880 | tf_op jit(solution)/shard_map/all_to_all | solution.py:152
  120.3 0.4 fusion.22
  120.7 0.1 copy_bitcast_fusion.2
  121.6 2.7 copy_bitcast_fusion.1
  124.3 113.8 %all-to-all-done.1 = bf16[8,512,320]{1,2,0:T(8,128)(2,1)} async-done(((bf16[8,512,320]{1,2,0:T(8,128)(2,1)}), bf16[8,512,320]{1,2,0:T(8,128)(2,1)}, u32[]{:S(2)}, u32[]{:S(2)}) %all-to-all-start.1) | async-done | bytes 2621472 | tf_op jit(solution)/shard_map/all_to_all | solution.py:152
  238.2 5.3 all-to-all-start.4
  243.4 2.3 copy.51
  245.7 1.8 fusion.4
  247.5 1.7 fusion.6
  249.3 2.4 copy.69
  251.7 0.9 fusion.25
  252.6 52.6 %all-to-all-done.4 = f32[8,128,320]{1,2,0:T(8,128)} async-done(((f32[8,128,320]{1,2,0:T(8,128)}), f32[8,128,320]{1,2,0:T(8,128)}, u32[]{:S(2)}, u32[]{:S(2)}) %all-to-all-start.4) | async-done | bytes 1310752 | tf_op jit(solution)/shard_map/all_to_all | solution.py:193
  305.3 0.6 broadcast_in_dim.13
  305.9 5.7 %all-to-all-start.2 = ((f32[64,2,128]{2,1,0:T(2,128)}), f32[64,2,128]{2,1,0:T(2,128)S(1)}, u32[]{:S(2)}, u32[]{:S(2)}) async-start(f32[64,2,128]{2,1,0:T(2,128)} %broadcast_in_dim.13), calls=%async_computation.2 | async-start | bytes 131072 | tf_op jit(solution)/shard_map/all_to_all | solution.py:152
  311.7 2.3 copy.52
  314.0 1.4 reduce_sum.103
  315.4 4.7 copy.53
  320.1 5.3 dot_general.17
  325.4 3.2 all-to-all-done.2
  329.1 0.1 multiply_convert_fusion
  329.2 3.2 fusion.2
  332.4 0.2 copy.76
  332.7 6.3 %all_to_all.64 = f32[2,32,128,64]{2,3,1,0:T(8,128)} all-to-all(f32[2,32,128,64]{2,3,1,0:T(8,128)S(1)} %bitcast.66), channel_id=1, replica_groups=mesh['branch'=8,'tok_0'=4,'tok_1'=2,'tok_2'=4,'tok_3'=2] {'tok_3'}, dimensions={0} | all-to-all | bytes 4194304 | tf_op jit(solution)/shard_map/all_to_all | solution.py:193
  339.0 4.2 all-to-all-start
  343.3 2.8 reduce_sum.104
  346.1 47.9 %all-to-all-done = bf16[128,8,512]{2,0,1:T(8,128)(2,1)} async-done(((bf16[128,8,512]{2,0,1:T(8,128)(2,1)}), bf16[128,8,512]{2,0,1:T(8,128)(2,1)}, u32[]{:S(2)}, u32[]{:S(2)}) %all-to-all-start) | async-done | bytes 1048608 | tf_op jit(solution)/shard_map/all_to_all | solution.py:287
  394.0 59.3 %all_to_all.65 = f32[32,128,64]{1,2,0:T(8,128)} all-to-all(f32[32,128,64]{1,2,0:T(8,128)} %reduce_sum.104), channel_id=1, replica_groups=mesh['branch'=8,'tok_0'=4,'tok_1'=2,'tok_2'=4,'tok_3'=2] {'tok_0','tok_1..., dimensions={0} | all-to-all | bytes 2097152 | tf_op jit(solution)/shard_map/all_to_all | solution.py:212
  453.3 0.9 broadcast_in_dim.15
  454.2 14.5 %all-to-all-start.5 = ((bf16[8,128,320]{1,2,0:T(8,128)(2,1)}), bf16[8,128,320]{1,2,0:T(8,128)(2,1)S(1)}, u32[]{:S(2)}, u32[]{:S(2)}) async-start(bf16[8,128,320]{1,2,0:T(8,128)(2,1)} %broadcast_in_dim.15), calls=%async_computation.5 | async-start | bytes 1310720 | tf_op jit(solution)/shard_map/all_to_all | solution.py:152
  468.8 1.3 reduce_sum.105
  470.1 0.9 fusion.19
  471.0 21.8 %all-to-all-done.5 = bf16[8,128,320]{1,2,0:T(8,128)(2,1)S(1)} async-done(((bf16[8,128,320]{1,2,0:T(8,128)(2,1)}), bf16[8,128,320]{1,2,0:T(8,128)(2,1)S(1)}, u32[]{:S(2)}, u32[]{:S(2)}) %all-to-all-start.5) | async-done | bytes 655392 | tf_op jit(solution)/shard_map/all_to_all | solution.py:152
  492.8 22.7 %all_to_all.66 = f32[8,1,64]{2,1,0:T(1,128)S(1)} all-to-all(f32[8,1,64]{2,1,0:T(1,128)S(1)} %broadcast_in_dim.17), channel_id=1, replica_groups=mesh['branch'=8,'tok_0'=4,'tok_1'=2,'tok_2'=4,'tok_3'=2] {'branch'}, dimensions={0} | all-to-all | bytes 4096 | tf_op jit(solution)/shard_map/all_to_all | solution.py:152
  515.4 0.6 broadcast_in_dim.16
  516.1 8.1 %all-to-all-start.8 = ((f32[64,1,128]{2,1,0:T(1,128)}), f32[64,1,128]{2,1,0:T(1,128)S(1)}, u32[]{:S(2)}, u32[]{:S(2)}) async-start(f32[64,1,128]{2,1,0:T(1,128)} %broadcast_in_dim.16), calls=%async_computation.8 | async-start | bytes 65536 | tf_op jit(solution)/shard_map/all_to_all | solution.py:152
  524.1 2.6 convolution_bitcast_fusion
  526.7 0.5 reduce_sum.109
  527.2 13.3 %all-to-all-done.8 = f32[64,1,128]{2,1,0:T(1,128)S(1)} async-done(((f32[64,1,128]{2,1,0:T(1,128)}), f32[64,1,128]{2,1,0:T(1,128)S(1)}, u32[]{:S(2)}, u32[]{:S(2)}) %all-to-all-start.8) | async-done | bytes 32800 | tf_op jit(solution)/shard_map/all_to_all | solution.py:152
  540.6 1.4 fusion.16
  (78 shorter events, 1.4 us)
Async XLA Ops:
  0.6 61.0 %copy-start = (bf16[1,4096,320]{1,2,0:T(8,128)(2,1)S(1)}, bf16[1,4096,320]{1,2,0:T(8,128)(2,1)}, u32[]{:S(2)}) copy-start(bf16[1,4096,320]{1,2,0:T(8,128)(2,1)} %param.10) | copy-start | bytes 7864324
  67.0 1.1 copy-start.2
  67.0 38.3 %copy-start.3 = (bf16[512,320]{0,1:T(8,128)(2,1)S(1)}, bf16[512,320]{0,1:T(8,128)(2,1)}, u32[]{:S(2)}) copy-start(bf16[512,320]{0,1:T(8,128)(2,1)} %param.13) | copy-start | bytes 983044
  107.1 13.2 %copy-start.5 = (s32[1024,1]{0,1:T(1,128)S(1)}, s32[1024,1]{0,1:T(1,128)}, u32[]{:S(2)}) copy-start(s32[1024,1]{0,1:T(1,128)} %param.14) | copy-start | bytes 12292
  107.1 131.1 %all-to-all-start.1 = ((bf16[8,512,320]{1,2,0:T(8,128)(2,1)}), bf16[8,512,320]{1,2,0:T(8,128)(2,1)}, u32[]{:S(2)}, u32[]{:S(2)}) async-start(bf16[8,512,320]{1,2,0:T(8,128)(2,1)} %broadcast_in_dim.12), calls=%async_computation.1 | async-start | bytes 5242880 | tf_op jit(solution)/shard_map/all_to_all | solution.py:152
  238.2 67.1 %all-to-all-start.4 = ((f32[8,128,320]{1,2,0:T(8,128)}), f32[8,128,320]{1,2,0:T(8,128)}, u32[]{:S(2)}, u32[]{:S(2)}) async-start(f32[8,128,320]{1,2,0:T(8,128)} %copy_bitcast_fusion.1), calls=%async_computation.4 | async-start | bytes 2621440 | tf_op jit(solution)/shard_map/all_to_all | solution.py:193
  243.4 4.1 copy-start.4
  249.3 2.4 copy-start.1
  305.9 22.6 %all-to-all-start.2 = ((f32[64,2,128]{2,1,0:T(2,128)}), f32[64,2,128]{2,1,0:T(2,128)S(1)}, u32[]{:S(2)}, u32[]{:S(2)}) async-start(f32[64,2,128]{2,1,0:T(2,128)} %broadcast_in_dim.13), calls=%async_computation.2 | async-start | bytes 131072 | tf_op jit(solution)/shard_map/all_to_all | solution.py:152
  320.1 9.0 %copy-start.6 = (s32[128]{0:T(128)S(1)}, s32[128]{0:T(128)}, u32[]{:S(2)}) copy-start(s32[128]{0:T(128)} %param.15) | copy-start | bytes 1540
  339.0 55.0 %all-to-all-start = ((bf16[128,8,512]{2,0,1:T(8,128)(2,1)}), bf16[128,8,512]{2,0,1:T(8,128)(2,1)}, u32[]{:S(2)}, u32[]{:S(2)}) async-start(bf16[128,8,512]{2,0,1:T(8,128)(2,1)} %copy.52), calls=%async_computation | async-start | bytes 2097152 | tf_op jit(solution)/shard_map/all_to_all | solution.py:287
  454.2 38.5 %all-to-all-start.5 = ((bf16[8,128,320]{1,2,0:T(8,128)(2,1)}), bf16[8,128,320]{1,2,0:T(8,128)(2,1)S(1)}, u32[]{:S(2)}, u32[]{:S(2)}) async-start(bf16[8,128,320]{1,2,0:T(8,128)(2,1)} %broadcast_in_dim.15), calls=%async_computation.5 | async-start | bytes 1310720 | tf_op jit(solution)/shard_map/all_to_all | solution.py:152
  516.1 24.5 %all-to-all-start.8 = ((f32[64,1,128]{2,1,0:T(1,128)}), f32[64,1,128]{2,1,0:T(1,128)S(1)}, u32[]{:S(2)}, u32[]{:S(2)}) async-start(f32[64,1,128]{2,1,0:T(1,128)} %broadcast_in_dim.16), calls=%async_computation.8 | async-start | bytes 65536 | tf_op jit(solution)/shard_map/all_to_all | solution.py:152

commit v2 on v0

v2 whole, which is shorter than its diff:
```python
import jax
import jax.numpy as jnp
from jax import lax
from jax.experimental import pallas as pl
from jax.experimental.pallas import tpu as pltpu
from jax.sharding import Mesh
from jax.sharding import PartitionSpec as P

DEN = 64
eps = 1e-05
mix_label = 0.25
loss_scale = 64.0
width_of_model = 4096
MESH = pl.DeviceIdType.MESH
B, Y, H, X, C = "branch", "tok_0", "tok_1", "tok_2", "tok_3"
TOK = (Y, H, X, C)


def ring(value, step, size):
    return lax.rem(value + (step + size), size)


def gather_kernel(
    block_ref, head_ref, piece_ref, out_ref, heads_ref, slices_ref,
    local_sem, send_sem, recv_sem, head_send, head_recv, piece_send, piece_recv,
):
    b = lax.axis_index(B)
    y, h, x, c = (lax.axis_index(name) for name in TOK)
    barrier = pltpu.get_barrier_semaphore()
    peers = [
        {X: ring(x, 1, 4)}, {X: ring(x, -1, 4)}, {Y: ring(y, 1, 4)}, {Y: ring(y, -1, 4)},
        {H: 1 - h}, {C: 1 - c},
    ] + [{B: ring(b, step, 8)} for step in range(1, 8)]
    for peer in peers:
        pl.semaphore_signal(barrier, inc=1, device_id=peer, device_id_type=MESH)
    pl.semaphore_wait(barrier, len(peers))

    numbers = iter(range(128))
    sent = []
    last = []

    def remote(source, target, send, recv, peer):
        return pltpu.make_async_remote_copy(
            src_ref=source, dst_ref=target, send_sem=send, recv_sem=recv,
            device_id=peer, device_id_type=MESH,
        )

    def move(piece, peer, arriving, source=None):
        number = next(numbers)
        send, recv = send_sem.at[number], recv_sem.at[number]
        copy = remote(piece if source is None else source, piece, send, recv, peer)
        copy.start()
        sent.append(copy)
        return remote(arriving, arriving, send, recv, peer).wait_recv

    def route(ref, side, plane, source):
        half = ref.shape[-1] // 2
        start = side * half
        cols = pl.ds(start, half)
        quarters = (pl.ds(start, half // 2), pl.ds(start + half // 2, half // 2))
        axis, other = ((X, Y), (Y, X))[side]
        mine, theirs = ((x, y), (y, x))[side]
        every = pl.ds(0, 4)

        def near(step, cs):
            at = ring(mine, step, 4)
            return ref.at[y, plane, at, c, :, cs] if side == 0 else ref.at[at, plane, x, c, :, cs]

        def rows(step, core, cs):
            at = ring(theirs, step, 4)
            return ref.at[at, plane, every, core, :, cs] if side == 0 else ref.at[every, plane, at, core, :, cs]

        def share(step):
            last.append(move(rows(step, c, cols), {C: 1 - c}, rows(step, 1 - c, cols)))

        forth, back = {axis: ring(mine, 1, 4)}, {axis: ring(mine, -1, 4)}
        first = None if source is None else source.at[:, cols]
        up = move(near(0, cols), forth, near(-1, cols), first)
        down = move(near(0, cols), back, near(1, cols), first)
        yield
        up()
        far_up = move(near(-1, quarters[0]), forth, near(2, quarters[0]))
        down()
        far_down = move(near(1, quarters[1]), back, near(2, quarters[1]))
        yield
        far_up()
        far_down()
        forth, back = {other: ring(theirs, 1, 4)}, {other: ring(theirs, -1, 4)}
        up = move(rows(0, c, cols), forth, rows(-1, c, cols))
        down = move(rows(0, c, cols), back, rows(1, c, cols))
        share(0)
        yield
        up()
        far_up = move(rows(-1, c, quarters[0]), forth, rows(2, c, quarters[0]))
        down()
        far_down = move(rows(1, c, quarters[1]), back, rows(2, c, quarters[1]))
        share(-1)
        share(1)
        yield
        far_up()
        far_down()
        share(2)

    def head_copies(step):
        up = remote(
            head_ref if step == 0 else heads_ref.at[jnp.maximum(b - step, 0)], heads_ref.at[jnp.maximum(b - step, 0)],
            head_send.at[0, step], head_recv.at[0, step], {B: jnp.minimum(b + 1, 7)},
        )
        down = remote(
            head_ref if step == 0 else heads_ref.at[jnp.minimum(b + step, 7)], heads_ref.at[jnp.minimum(b + step, 7)],
            head_send.at[1, step], head_recv.at[1, step], {B: jnp.maximum(b - 1, 0)},
        )
        return (
            (up, jnp.logical_and(b < 7, b >= step), b >= step + 1),
            (down, jnp.logical_and(b > 0, b + step <= 7), b + step <= 6),
        )

    def head_start(step):
        for copy, sends, _ in head_copies(step):
            pl.when(sends)(copy.start)

    def head_arrive(step):
        for copy, _, receives in head_copies(step):
            pl.when(receives)(copy.wait_recv)

    def head_sent(step):
        for copy, sends, _ in head_copies(step):
            pl.when(sends)(copy.wait_send)

    def head_next(step):
        head_arrive(step - 1)
        head_start(step)

    own = pltpu.make_async_copy(block_ref, out_ref.at[y, h, x, c], local_sem.at[0])
    own_head = pltpu.make_async_copy(head_ref, heads_ref.at[b], local_sem.at[1])
    across = move(out_ref.at[y, h, x, c], {H: 1 - h}, out_ref.at[y, 1 - h, x, c], block_ref)
    own.start()

    def piece_at(slot):
        return slices_ref.at[y, h, x, c, :, pl.ds(pl.multiple_of(128 * slot, 128), 128)]

    slot = lax.rem(b, 4)
    gives = (b // 4) == c
    pieces = [
        remote(
            piece_ref.at[ring(b, step, 8)], piece_at(slot), piece_send.at[step - 1], piece_recv.at[slot],
            {B: ring(b, step, 8)},
        )
        for step in range(1, 8)
    ]
    own_piece = pltpu.make_async_copy(piece_ref.at[b], piece_at(slot), local_sem.at[2])

    @pl.when(gives)
    def _():
        own_piece.start()
        for piece in pieces:
            piece.start()

    def pieces_arrive():
        for number in range(4):
            arriving = remote(
                piece_at(number), piece_at(number), piece_send.at[0], piece_recv.at[number], {B: ring(b, 1, 8)}
            )
            pl.when(b != 4 * c + number)(arriving.wait_recv)

        @pl.when(gives)
        def _():
            own_piece.wait()

    routes = [route(out_ref, 0, h, block_ref), route(out_ref, 1, h, block_ref)]
    late = [route(out_ref, 0, 1 - h, None), route(out_ref, 1, 1 - h, None)]
    thin = [route(slices_ref, 0, h, None), route(slices_ref, 1, h, None)]
    thin_late = [route(slices_ref, 0, 1 - h, None), route(slices_ref, 1, 1 - h, None)]

    def go(*groups):
        for group in groups:
            for r in group:
                next(r, None)

    go(routes)
    head_start(0)
    own_head.start()
    go(routes)
    pieces_arrive()
    thin_across = move(slices_ref.at[y, h, x, c], {H: 1 - h}, slices_ref.at[y, 1 - h, x, c])
    own.wait()
    go(routes, thin)
    head_next(1)
    go(routes, thin)
    across()
    go(late, routes, thin)
    head_next(2)
    thin_across()
    go(late, thin, thin_late)
    go(late, thin, thin_late)
    head_next(3)
    go(late, thin_late)
    head_next(4)
    go(late, thin_late)
    go(thin_late)
    head_next(5)
    head_next(6)
    head_arrive(6)
    own_head.wait()
    for arrive in last:
        arrive()
    for copy in sent:
        copy.wait_send()
    for step in range(7):
        head_sent(step)

    @pl.when(gives)
    def _():
        for piece in pieces:
            piece.wait_send()


def gather_all(block, head, pieces):
    rows, width = block.shape
    anywhere = pl.BlockSpec(memory_space=pl.ANY)
    return pl.pallas_call(
        gather_kernel,
        out_shape=(
            jax.ShapeDtypeStruct((4, 2, 4, 2, rows, width), block.dtype),
            jax.ShapeDtypeStruct((8, *head.shape), head.dtype),
            jax.ShapeDtypeStruct((4, 2, 4, 2, 16, 512), pieces.dtype),
        ),
        in_specs=[anywhere] * 3,
        out_specs=(anywhere,) * 3,
        scratch_shapes=[
            pltpu.SemaphoreType.DMA((3,)),
            pltpu.SemaphoreType.DMA((128,)),
            pltpu.SemaphoreType.DMA((128,)),
            pltpu.SemaphoreType.DMA((2, 7)),
            pltpu.SemaphoreType.DMA((2, 7)),
            pltpu.SemaphoreType.DMA((7,)),
            pltpu.SemaphoreType.DMA((4,)),
        ],
        compiler_params=pltpu.CompilerParams(collective_id=0, has_side_effects=True),
        name="gather_all",
    )(block, head, pieces)


def normalize(hidden, gain):
    values = hidden.astype(jnp.float32)
    inv_scale = lax.rsqrt(jnp.mean(values * values, axis=-1, keepdims=True) + eps)
    return ((values * inv_scale * gain).astype(jnp.bfloat16), inv_scale)


def finish_kernel(
    terms_ref, stats_ref, weight_ref, normed_ref, label_ref, heads_ref, hidden_ref, gain_ref,
    cols_ref, cols_gain_ref, inv_ref,
    grads_ref, hidden_out_ref, gain_out_ref,
    got_terms, near_stats, far_stats, factor, got_factor, grads, own_part, give_part, got_part,
    plane_give, plane_got, dots, dots_near, dots_far, piece, halves, sums, got_sums,
    local_sem, term_send, term_recv, near_send, near_recv, far_send, far_recv, factor_send, factor_recv,
    grad_send, grad_recv, part_send, part_recv, plane_send, plane_recv, dots_send, dots_recv,
    dot_near_send, dot_near_recv, half_send, half_recv, sum_send, sum_recv,
):
    b = lax.axis_index(B)
    y, h, x, c = (lax.axis_index(name) for name in TOK)
    along = [{B: ring(b, step, 8)} for step in range(1, 8)]
    near = [{H: h, C: 1 - c}, {H: 1 - h, C: c}, {H: 1 - h, C: 1 - c}]
    plane = [(dy, dx) for dy in range(4) for dx in range(4) if dy or dx]
    there = [{Y: ring(y, dy, 4), X: ring(x, dx, 4)} for dy, dx in plane]

    barrier = pltpu.get_barrier_semaphore()
    for peer in along + near + there:
        pl.semaphore_signal(barrier, inc=1, device_id=peer, device_id_type=MESH)
    pl.semaphore_wait(barrier, len(along) + len(near) + len(there))
    sent = []

    def move(source, target, send, recv, peer):
        copy = pltpu.make_async_remote_copy(
            src_ref=source, dst_ref=target, send_sem=send, recv_sem=recv, device_id=peer, device_id_type=MESH
        )
        copy.start()
        sent.append(copy)

    def arrive(target, send, recv, peer):
        pltpu.make_async_remote_copy(
            src_ref=target, dst_ref=target, send_sem=send, recv_sem=recv, device_id=peer, device_id_type=MESH
        ).wait_recv()

    def spread(source_of, target, send, recv):
        for n, peer in enumerate(along):
            move(source_of(peer[B]), target.at[b], send.at[n], recv.at[n], peer)

    def collect(target, send, recv):
        for n in range(7):
            arrive(target.at[ring(b, -(n + 1), 8)], send.at[n], recv.at[n], along[n])

    own_terms = pltpu.make_async_copy(terms_ref.at[b], got_terms.at[b], local_sem.at[0])
    own_terms.start()
    spread(lambda at: terms_ref.at[at], got_terms, term_send, term_recv)

    def add_block(q, total):
        columns = normed_ref[:, pl.ds(pl.multiple_of(q * 512, 512), 512)]
        return total + lax.dot_general(
            heads_ref[q], columns, (((1,), (1,)), ((), ())), preferred_element_type=jnp.float32
        )

    logits = lax.fori_loop(0, 8, add_block, jnp.zeros((320, 128), jnp.float32))
    local_top = jnp.max(logits, axis=0, keepdims=True)
    scaled = jnp.exp(logits - local_top)
    stats_ref_own = near_stats.at[0]
    stats_ref_own[...] = stats_ref[...]
    near_stats[0, 0, 8:9, :] = local_top
    near_stats[0, 1, 8:9, :] = jnp.sum(scaled, axis=0, keepdims=True)
    for n, peer in enumerate(near):
        move(near_stats.at[0], near_stats.at[n + 1], near_send.at[n], near_recv.at[n], peer)
    for n, peer in enumerate(near):
        arrive(near_stats.at[n + 1], near_send.at[n], near_recv.at[n], peer)

    def joined(stats, count):
        top = stats[0, 0]
        for n in range(1, count):
            top = jnp.maximum(top, stats[n, 0])
        total = jnp.zeros_like(top)
        for n in range(count):
            total += stats[n, 1] * jnp.exp(stats[n, 0] - top)
        return top, total

    top, total = joined(near_stats, 4)
    far_stats[0, 0] = top
    far_stats[0, 1] = total
    for n, peer in enumerate(there):
        move(far_stats.at[0], far_stats.at[n + 1], far_send.at[n], far_recv.at[n], peer)
    for n, peer in enumerate(there):
        arrive(far_stats.at[n + 1], far_send.at[n], far_recv.at[n], peer)
    top, total = joined(far_stats, 16)
    ratio = jnp.exp(near_stats[0, 0] - top) / total
    factor[...] = ratio[0:8] * weight_ref[...]
    own_ratio = ratio[8:9]
    got_factor[b] = factor[...]
    spread(lambda at: factor, got_factor, factor_send, factor_recv)
    collect(got_factor, factor_send, factor_recv)
    collect(got_terms, term_send, term_recv)
    own_terms.wait()

    def add_branch(n, mixed):
        return mixed + got_terms[n].astype(jnp.float32) * got_factor[n, pl.ds(b, 1), :]

    mixed = lax.fori_loop(0, 8, add_branch, jnp.zeros((320, 128), jnp.float32))
    targets = (1.0 - mix_label) * mixed + mix_label * label_ref[...]
    grads[...] = (loss_scale * (scaled * own_ratio - targets)).astype(jnp.bfloat16)
    own_grads = pltpu.make_async_copy(grads, grads_ref.at[b], local_sem.at[1])
    own_grads.start()
    spread(lambda at: grads, grads_ref, grad_send, grad_recv)

    def part(q):
        result = lax.dot_general(
            grads[...], heads_ref[q], (((0,), (0,)), ((), ())), preferred_element_type=jnp.float32
        )
        columns = pl.ds(pl.multiple_of(q * 512, 512), 512)
        weighted = hidden_ref[:, columns].astype(jnp.float32) * gain_ref[:, columns]
        return result, jnp.sum(result * weighted, axis=1, keepdims=True)

    column_dots = jnp.zeros((128, 1), jnp.float32)
    for n in range(4):
        result, dot = part(2 * n + (1 - c))
        give_part[n] = result
        column_dots += dot
        move(give_part.at[n], got_part.at[n], part_send.at[n], part_recv.at[n], {C: 1 - c})
    for n in range(4):
        result, dot = part(2 * n + c)
        own_part[n] = result
        column_dots += dot
    dots[0] = jnp.broadcast_to(column_dots, (128, 128)).T[0:8]
    for n, peer in enumerate(there):
        move(dots.at[0], dots_far.at[n], dots_send.at[n], dots_recv.at[n], peer)
    for n in range(4):
        arrive(got_part.at[n], part_send.at[n], part_recv.at[n], {C: 1 - c})
        both = own_part[n] + got_part[n]
        for m in range(4):
            plane_give[n, m] = both[:, 128 * m : 128 * m + 128].astype(jnp.bfloat16)
    for n, peer in enumerate(there):
        move(plane_give.at[peer[Y], peer[X]], plane_got.at[n], plane_send.at[n], plane_recv.at[n], peer)
    row_dots = dots[0]
    for n, peer in enumerate(there):
        arrive(dots_far.at[n], dots_send.at[n], dots_recv.at[n], peer)
        row_dots += dots_far[n]
    dots_near[0] = row_dots
    for n, peer in enumerate(near):
        move(dots_near.at[0], dots_near.at[n + 1], dot_near_send.at[n], dot_near_recv.at[n], peer)
    block = plane_give[y, x].astype(jnp.float32)
    for n, peer in enumerate(there):
        arrive(plane_got.at[n], plane_send.at[n], plane_recv.at[n], peer)
        block += plane_got[n].astype(jnp.float32)
    turned = block.T
    piece[0] = turned[0:64]
    piece[1] = turned[64:128]
    for core in range(2):
        mine = jnp.logical_and(h == c, c == core)
        copy = pltpu.make_async_remote_copy(
            src_ref=piece.at[core], dst_ref=halves.at[h], send_sem=half_send.at[core], recv_sem=half_recv.at[h],
            device_id={H: c, C: core}, device_id_type=MESH,
        )

        @pl.when(jnp.logical_not(mine))
        def _():
            copy.start()

        @pl.when(mine)
        def _():
            halves[h] = piece[core]

    for n, peer in enumerate(near):
        arrive(dots_near.at[n + 1], dot_near_send.at[n], dot_near_recv.at[n], peer)
    row_dot = (dots_near[0] + dots_near[1] + dots_near[2] + dots_near[3])[0:1]
    for source in range(2):
        waits = pltpu.make_async_remote_copy(
            src_ref=halves.at[source], dst_ref=halves.at[source], send_sem=half_send.at[0],
            recv_sem=half_recv.at[source], device_id={C: 1 - c}, device_id_type=MESH,
        )
        pl.when(jnp.logical_not(jnp.logical_and(h == source, c == h)))(waits.wait_recv)
    normed_grads = halves[0] + halves[1]
    inv_scale = inv_ref[...]
    values = cols_ref[...]
    terms = normed_grads * values * inv_scale
    sums[...] = jnp.broadcast_to(
        jnp.sum(jnp.concatenate([terms, terms], axis=0).T, axis=0, keepdims=True), (8, 128)
    )
    got_sums[b] = sums[...]
    spread(lambda at: sums, got_sums, sum_send, sum_recv)
    hidden_out_ref[...] = (
        inv_scale * cols_gain_ref[...] * normed_grads - values * inv_scale**3 * row_dot / width_of_model
    )
    collect(grads_ref, grad_send, grad_recv)
    own_grads.wait()
    collect(got_sums, sum_send, sum_recv)
    gain = got_sums[0]
    for n in range(1, 8):
        gain += got_sums[n]
    gain_out_ref[...] = gain
    for copy in sent:
        copy.wait_send()
    for core in range(2):
        mine = jnp.logical_and(h == c, c == core)
        copy = pltpu.make_async_remote_copy(
            src_ref=piece.at[core], dst_ref=halves.at[h], send_sem=half_send.at[core], recv_sem=half_recv.at[h],
            device_id={H: c, C: core}, device_id_type=MESH,
        )
        pl.when(jnp.logical_not(mine))(copy.wait_send)


def finish(*operands):
    inside = pl.BlockSpec(memory_space=pltpu.VMEM)
    anywhere = pl.BlockSpec(memory_space=pl.ANY)
    f32, bf16 = jnp.float32, jnp.bfloat16
    dma = pltpu.SemaphoreType.DMA
    pairs = [7, 3, 15, 7, 7, 4, 15, 15, 3, 2, 7]
    return pl.pallas_call(
        finish_kernel,
        out_shape=(
            jax.ShapeDtypeStruct((8, 320, 128), bf16),
            jax.ShapeDtypeStruct((64, 128), f32),
            jax.ShapeDtypeStruct((8, 128), f32),
        ),
        in_specs=[inside] * len(operands),
        out_specs=(anywhere, inside, inside),
        scratch_shapes=[
            pltpu.VMEM((8, 320, 128), bf16),
            pltpu.VMEM((4, 2, 16, 128), f32),
            pltpu.VMEM((16, 2, 16, 128), f32),
            pltpu.VMEM((8, 128), f32),
            pltpu.VMEM((8, 8, 128), f32),
            pltpu.VMEM((320, 128), bf16),
            pltpu.VMEM((4, 128, 512), f32),
            pltpu.VMEM((4, 128, 512), f32),
            pltpu.VMEM((4, 128, 512), f32),
            pltpu.VMEM((4, 4, 128, 128), bf16),
            pltpu.VMEM((15, 128, 128), bf16),
            pltpu.VMEM((1, 8, 128), f32),
            pltpu.VMEM((4, 8, 128), f32),
            pltpu.VMEM((15, 8, 128), f32),
            pltpu.VMEM((2, 64, 128), f32),
            pltpu.VMEM((2, 64, 128), f32),
            pltpu.VMEM((8, 128), f32),
            pltpu.VMEM((8, 8, 128), f32),
            dma((2,)),
        ] + [dma((n,)) for n in pairs for _ in range(2)],
        compiler_params=pltpu.CompilerParams(collective_id=1, has_side_effects=True, vmem_limit_bytes=48 << 20),
        name="finish",
    )(*operands)


def per_device(
    teacher_hidden, teacher_gain, teacher_head, student_hidden, student_gain, student_head, cluster_weights, token_ids
):
    cols = student_head.shape[1]
    place = lax.axis_index(TOK)
    own_normed, _ = normalize(teacher_hidden[0], teacher_gain[0])
    student_normed, inv_scale = normalize(student_hidden, student_gain)
    four = lax.dynamic_slice_in_dim(student_normed, 4 * (place // 2), 4, 0)
    pieces = four.reshape(4, 8, 512).transpose(1, 0, 2).reshape(8, 16, 128)
    normed, heads, slices = gather_all(own_normed, student_head.T, pieces)
    normed = normed.reshape(1024, 4096)
    logits = lax.dot_general(
        teacher_head[0].T, normed, (((1,), (1,)), ((), ())), preferred_element_type=jnp.float32
    )
    top = jnp.max(logits, axis=0)
    scaled = jnp.exp(logits - top)
    total = jnp.sum(scaled, axis=0)
    terms = scaled.astype(jnp.bfloat16).reshape(320, 8, 128).transpose(1, 0, 2)
    stats = jnp.pad(jnp.stack([top.reshape(8, 128), total.reshape(8, 128)]), ((0, 0), (0, 8), (0, 0)))
    weight = (cluster_weights[:, 0].astype(jnp.float32) / DEN).reshape(8, 128)
    offset = place * cols
    label = (token_ids[None, :] == offset + jnp.arange(cols, dtype=jnp.int32)[:, None]).astype(jnp.float32)
    hidden_cols = lax.dynamic_slice_in_dim(student_hidden, place * 64, 64, 1).astype(jnp.float32).T
    gain_cols = lax.dynamic_slice_in_dim(student_gain, place * 64, 64, 0)
    grads, grad_hidden, grad_gain = finish(
        terms, stats, weight, student_normed, label, heads, student_hidden, student_gain[None, :],
        hidden_cols, jnp.broadcast_to(gain_cols[:, None], (64, 128)), inv_scale.reshape(1, 128),
    )
    slices = slices.reshape(32, 2, 16, 4, 128).transpose(1, 3, 0, 2, 4).reshape(8, 128, 512)
    grad_head = lax.dot_general(
        grads, slices, (((0, 2), (0, 1)), ((), ())), preferred_element_type=jnp.float32
    )
    return (grad_head.T, grad_hidden.T, grad_gain[0, :64])


def solution(mesh):
    split = Mesh(mesh.devices.reshape(mesh.shape["branch"], 4, 2, 4, 2), (B, *TOK))
    in_specs = (
        P("branch", TOK, None), P("branch", None), P("branch", None, TOK), P("branch", None), P(),
        P("branch", TOK), P(None, "branch"), P("branch"),
    )
    out_specs = (P("branch", TOK), P("branch", TOK), P(TOK))
    return jax.shard_map(per_device, mesh=split, in_specs=in_specs, out_specs=out_specs, check_vma=False)
```

time: 603 us -> 207 us (0.34)
  waiting for transfers between devices: 381 us -> 0 us
  Pallas kernels: 0 us -> 179 us
  blocking collectives: 81.7 us -> 0 us
  starting transfers between devices: 66.6 us -> 0 us
  other arithmetic: 21.5 us -> 4.52 us
  between operations: 14.4 us -> 0.86 us
  local copies, waits for them, and re-layouts: 26.8 us -> 14.3 us
    all_gather x1 -> x0, waiting for transfers between devices: 211 us -> none  [per_device(): lax.all_gather(teacher_hidden[0], TOK, axis=0, tiled=True)]
    pallas_call x0 -> x2, Pallas kernels: none -> 179 us  [the longest x1 94.6 us: finish(): pl.pallas_call(finish_kernel, out_shape=(jax.ShapeDtypeStruct((8, 320, 12...]
    all_to_all x7 -> x0, waiting for transfers between devices: 170 us -> none  [the longest x5 72.7 us: copy_for_each(): return lax.all_to_all(copies, axis, split_axis=0, concat_axis=0, tiled=True)]
    all_to_all x3 -> x0, blocking collectives: 81.7 us -> none  [the longest x1 51.6 us: summed_rows(): lax.all_to_all(nearer, far, split_axis=0, concat_axis=0, tiled=True)]
    all_to_all x7 -> x0, starting transfers between devices: 66.6 us -> none  [the longest x5 48.7 us: copy_for_each(): return lax.all_to_all(copies, axis, split_axis=0, concat_axis=0, tiled=True)]
    reduce_sum x8 -> x1, other arithmetic: 7.28 us -> 0.24 us  [per_device(): total = jnp.sum(scaled, axis=0)]
    all_to_all x2 -> x0, local copies, waits for them, and re-layouts: 6.95 us -> none  [the longest x1 4.7 us: copy_for_each(): return lax.all_to_all(copies, axis, split_axis=0, concat_axis=0, tiled=True)]
  transfers between devices with their start and end apart: 8 -> 0, of which waited for: 7 -> 0; matrix products, arithmetic and copies ran while one was open for 8% -> 0% of each run, Pallas kernels for 0% -> 0%
where the time goes in v2:
time: 207 us
  Pallas kernels  179 us (86%)
  local copies, waits for them, and re-layouts  14.3 us (7%)
  matrix products  7.9 us (4%)
  other arithmetic  4.52 us (2%)
    pallas_call x1, Pallas kernels, finish(): pl.pallas_call(finish_kernel, out_shape=(jax.ShapeDtypeStruct((8, 320, 12...  94.6 us
    pallas_call x1, Pallas kernels, gather_all(): pl.pallas_call(gather_kernel, out_shape=(jax.ShapeDtypeStruct((4, 2, 4, 2...  84.6 us
    dot_general x1, matrix products, per_device(): lax.dot_general(teacher_head[0].T, normed, (((1,), (1,)), ((), ())), pref...  5.34 us
    unnamed x24, local copies, waits for them, and re-layouts  5.01 us
    reshape x2, local copies, waits for them, and re-layouts, per_device(): slices.reshape(32, 2, 16, 4, 128).transpose(1, 3, 0, 2, 4)  4.61 us

profile of v2, /device:TPU:1, one launch (start us, length us, event | category | flops | bytes accessed | tf_op | source)
XLA Modules:
  0.0 206.8 jit_solution(8680682487157184691)
XLA Ops:
  0.6 0.0 copy-start
  0.6 0.0 copy-start.7
  0.7 0.0 copy-start.8
  0.7 1.7 fusion.2
  2.4 1.6 fusion.4.normed_ref
  4.0 0.0 copy-start.2
  4.0 1.0 copy-done.2
  5.0 0.6 reshape.76.piece_ref
  5.6 0.0 copy-done.7
  5.6 0.1 fusion.8
  5.8 0.0 copy-done.8
  5.8 0.8 fusion.10.block_ref
  6.5 84.6 %gather_all.1 = (bf16[4,2,4,2,16,4096]{5,4,3,2,1,0:T(8,128)(2,1)}, bf16[8,320,512]{2,1,0:T(8,128)(2,1)}, bf16[4,2,4,2,16,512]{5,4,3,2,1,0:T(8,128)(2,1)}) custom-call(bf16[16,4096]{1,0:T(8,128)(2,1)} %fusion.10.block_ref, bf16[320,512]{1,0:T(8,128)(2,1)} %bitcast.50, bf16[8,16,128]{2,1,0:T(8,128)(2,1)} %reshape.76.piece_ref), custom_call_target="tpu_custom_call" | custom-call | tf_op jit(solution)/shard_map/gather_all/pallas_call | solution.py:221
  91.1 0.0 copy-done
  91.2 5.3 %fusion.12 = (f32[1024]{0:T(1024)S(1)}, f32[1024,320]{0,1:T(8,128)S(1)}) fusion(bf16[1024,4096]{1,0:T(8,128)(2,1)} %bitcast.55, bf16[1,4096,320]{1,2,0:T(8,128)(2,1)S(1)} %copy-done), kind=kOutput, calls=%fused_computation.30 | convolution fusion | flops 2684681216 | bytes 12324864 | tf_op jit(solution)/shard_map/dot_general | solution.py:499
  96.5 0.0 copy-start.6
  96.5 0.0 copy-start.10
  96.5 0.0 copy-start.9
  96.5 0.2 fusion.5
  96.8 0.1 copy.19
  96.9 0.8 constant_dynamic-slice_fusion
  97.8 0.1 copy.16
  97.9 0.0 copy-done.6
  97.9 0.1 dynamic_slice.11
  98.0 0.1 broadcast_in_dim.5.cols_gain_ref
  98.0 0.0 copy-done.10
  98.1 0.1 compare_convert_fusion.label_ref
  98.2 0.0 copy-done.9
  98.2 0.0 copy-start.1
  98.2 1.2 copy-done.1
  99.4 0.0 copy-start.3
  99.4 1.2 copy-done.3
  100.6 94.6 %finish.1 = (bf16[8,320,128]{2,1,0:T(8,128)(2,1)S(1)}, f32[64,128]{1,0:T(8,128)S(1)}, f32[8,128]{1,0:T(8,128)S(1)}) custom-call(bf16[8,320,128]{2,1,0:T(8,128)(2,1)S(1)} %bitcast.45, f32[2,16,128]{2,1,0:T(8,128)S(1)} %select_maximum_fusion.stats_ref, f32[8,128]{1,0:T(8,128)S(1)} %bitcast.48, bf16[128,4096]{1,0:T(8,128)(2,1)S(1)} %copy-done.3, ...), custom_call_target="tpu_custom_call" | custom-call | tf_op jit(solution)/shard_map/finish/pallas_call | solution.py:453
  195.3 0.0 copy-start.4
  195.3 0.8 copy-done.4
  196.1 2.1 %reshape.77 = bf16[32,2,16,4,128]{4,3,2,1,0:T(4,128)(2,1)} reshape(bf16[4,2,4,2,16,512]{5,4,3,2,1,0:T(8,128)(2,1)} %get-tuple-element.9) | data formatting | bytes 2097152 | tf_op jit(solution)/shard_map/reshape | solution.py:516
  198.2 0.0 copy-start.5
  198.2 2.4 %copy.13 = bf16[2,4,32,16,128]{4,3,2,1,0:T(8,128)(2,1)} copy(bf16[2,4,32,16,128]{4,1,3,0,2:T(4,128)(2,1)} %bitcast.49) | data formatting | bytes 2097152 | tf_op jit(solution)/shard_map/transpose | solution.py:516
  200.7 2.5 %reshape.78 = bf16[8,128,512]{2,1,0:T(8,128)(2,1)} reshape(bf16[2,4,32,16,128]{4,3,2,1,0:T(8,128)(2,1)} %copy.13) | data formatting | bytes 2097152 | tf_op jit(solution)/shard_map/reshape | solution.py:516
  203.1 0.0 copy-done.5
  203.2 2.6 %convolution_bitcast_fusion = f32[512,320]{0,1:T(8,128)} fusion(bf16[8,320,128]{2,1,0:T(8,128)(2,1)S(1)} %copy-done.5, bf16[8,128,512]{2,1,0:T(8,128)(2,1)} %reshape.78), kind=kOutput, calls=%fused_computation.8 | convolution fusion | flops 335544320 | bytes 2359296 | tf_op jit(solution)/shard_map/dot_general | solution.py:517
  205.7 0.5 slice_bitcast_fusion
  206.2 0.6 copy.21
  (7 shorter events, 0.1 us)
Async XLA Ops:
  0.6 90.5 %copy-start = (bf16[1,4096,320]{1,2,0:T(8,128)(2,1)S(1)}, bf16[1,4096,320]{1,2,0:T(8,128)(2,1)}, u32[]{:S(2)}) copy-start(bf16[1,4096,320]{1,2,0:T(8,128)(2,1)} %param.10) | copy-start | bytes 7864324
  0.6 5.0 %copy-start.7 = (bf16[1,16,4096]{2,1,0:T(8,128)(2,1)S(1)}, bf16[1,16,4096]{2,1,0:T(8,128)(2,1)}, u32[]{:S(2)}) copy-start(bf16[1,16,4096]{2,1,0:T(8,128)(2,1)} %param.8) | copy-start | bytes 393220
  0.7 5.1 %copy-start.8 = (f32[1,4096]{1,0:T(1,128)S(1)}, f32[1,4096]{1,0:T(1,128)}, u32[]{:S(2)}) copy-start(f32[1,4096]{1,0:T(1,128)} %param.9) | copy-start | bytes 49156
  4.0 1.0 copy-start.2
  96.5 1.4 copy-start.6
  96.5 1.5 copy-start.10
  96.5 1.6 copy-start.9
  98.2 1.2 copy-start.1
  99.4 1.2 copy-start.3
  195.3 0.8 copy-start.4
  198.2 4.9 %copy-start.5 = (bf16[8,320,128]{2,1,0:T(8,128)(2,1)S(1)}, bf16[8,320,128]{2,1,0:T(8,128)(2,1)}, u32[]{:S(2)}) copy-start(bf16[8,320,128]{2,1,0:T(8,128)(2,1)} %copy-done.4) | copy-start | bytes 1966084

commit v3 on v0

v3 whole, which is shorter than its diff:
```python
import jax
import jax.numpy as jnp
from jax import lax
from jax.experimental import pallas as pl
from jax.experimental.pallas import tpu as pltpu
from jax.sharding import Mesh
from jax.sharding import PartitionSpec as P

DEN = 64
eps = 1e-05
mix_label = 0.25
loss_scale = 64.0
width_of_model = 4096
MESH = pl.DeviceIdType.MESH
B, Y, H, X, C = "branch", "tok_0", "tok_1", "tok_2", "tok_3"
TOK = (Y, H, X, C)


def ring(value, step, size):
    return lax.rem(value + (step + size), size)


def kernel(
    hidden_block_ref, teacher_gain_ref, teacher_head_ref, hidden_ref, gain_ref, head_ref,
    weight_ref, label_ref, cols_ref, cols_gain_ref,
    grad_head_ref, hidden_out_ref, gain_out_ref,
    states, head_cols, heads, normed, slices, joined_slices, inv_cols,
    terms, got_terms, near_stats, far_stats, near_student, far_student, factor, got_factor, all_grads,
    own_part, give_part, got_part, plane_give, plane_got, dots, dots_near, dots_far, piece, halves, sums, got_sums,
    local_sem, send_sem, recv_sem, head_send, head_recv, piece_send, piece_recv,
    term_send, term_recv, near_send, near_recv, far_send, far_recv,
    student_near_send, student_near_recv, student_far_send, student_far_recv, factor_send, factor_recv,
    grad_send, grad_recv, part_send, part_recv, plane_send, plane_recv, dots_send, dots_recv,
    dot_near_send, dot_near_recv, half_send, half_recv, sum_send, sum_recv,
):
    b = lax.axis_index(B)
    y, h, x, c = (lax.axis_index(name) for name in TOK)
    along = [{B: ring(b, step, 8)} for step in range(1, 8)]
    near = [{H: h, C: 1 - c}, {H: 1 - h, C: c}, {H: 1 - h, C: 1 - c}]
    plane = [(dy, dx) for dy in range(4) for dx in range(4) if dy or dx]
    there = [{Y: ring(y, dy, 4), X: ring(x, dx, 4)} for dy, dx in plane]

    barrier = pltpu.get_barrier_semaphore()
    for peer in near + along + there:
        pl.semaphore_signal(barrier, inc=1, device_id=peer, device_id_type=MESH)
    own_teacher_head = pltpu.make_async_copy(teacher_head_ref, head_cols, local_sem.at[0])
    own_teacher_head.start()
    own_head = pltpu.make_async_copy(head_ref, heads.at[b], local_sem.at[1])
    own_head.start()

    def unit_rows(hidden, gain):
        values = hidden.astype(jnp.float32)
        inv_scale = lax.rsqrt(jnp.mean(values * values, axis=-1, keepdims=True) + eps)
        return (values * inv_scale * gain).astype(jnp.bfloat16), inv_scale

    states[y, h, x, c] = unit_rows(hidden_block_ref[...], teacher_gain_ref[...])[0]
    pl.semaphore_wait(barrier, len(near) + len(along) + len(there))

    numbers = iter(range(128))
    sent = []

    def remote(source, target, send, recv, peer):
        return pltpu.make_async_remote_copy(
            src_ref=source, dst_ref=target, send_sem=send, recv_sem=recv, device_id=peer, device_id_type=MESH
        )

    def move(source, target, send, recv, peer):
        copy = remote(source, target, send, recv, peer)
        copy.start()
        sent.append(copy)

    def arrive(target, send, recv, peer):
        remote(target, target, send, recv, peer).wait_recv()

    def step_of(part, peer, arriving):
        number = next(numbers)
        send, recv = send_sem.at[number], recv_sem.at[number]
        move(part, part, send, recv, peer)
        return remote(arriving, arriving, send, recv, peer).wait_recv

    def spread(source_of, target, send, recv):
        for n, peer in enumerate(along):
            move(source_of(peer[B]), target.at[b], send.at[n], recv.at[n], peer)

    def collect(target, send, recv):
        for n in range(7):
            arrive(target.at[ring(b, -(n + 1), 8)], send.at[n], recv.at[n], along[n])

    def route(ref, side, layer, shared):
        half = ref.shape[-1] // 2
        start = side * half
        cols = pl.ds(start, half)
        quarters = (pl.ds(start, half // 2), pl.ds(start + half // 2, half // 2))
        axis, other = ((X, Y), (Y, X))[side]
        mine, theirs = ((x, y), (y, x))[side]
        every = pl.ds(0, 4)

        def beside(step, cs):
            at = ring(mine, step, 4)
            return ref.at[y, layer, at, c, :, cs] if side == 0 else ref.at[at, layer, x, c, :, cs]

        def rows(step, core, cs):
            at = ring(theirs, step, 4)
            return ref.at[at, layer, every, core, :, cs] if side == 0 else ref.at[every, layer, at, core, :, cs]

        def share(step):
            shared.append(step_of(rows(step, c, cols), {C: 1 - c}, rows(step, 1 - c, cols)))

        forth, back = {axis: ring(mine, 1, 4)}, {axis: ring(mine, -1, 4)}
        up = step_of(beside(0, cols), forth, beside(-1, cols))
        down = step_of(beside(0, cols), back, beside(1, cols))
        yield
        up()
        far_up = step_of(beside(-1, quarters[0]), forth, beside(2, quarters[0]))
        down()
        far_down = step_of(beside(1, quarters[1]), back, beside(2, quarters[1]))
        yield
        far_up()
        far_down()
        forth, back = {other: ring(theirs, 1, 4)}, {other: ring(theirs, -1, 4)}
        up = step_of(rows(0, c, cols), forth, rows(-1, c, cols))
        down = step_of(rows(0, c, cols), back, rows(1, c, cols))
        share(0)
        yield
        up()
        far_up = step_of(rows(-1, c, quarters[0]), forth, rows(2, c, quarters[0]))
        down()
        far_down = step_of(rows(1, c, quarters[1]), back, rows(2, c, quarters[1]))
        share(-1)
        share(1)
        yield
        far_up()
        far_down()
        share(2)

    def head_copies(step, part):
        rows = pl.ds(160 * part, 160)
        low, high = jnp.maximum(b - step, 0), jnp.minimum(b + step, 7)
        up = remote(
            (head_ref if step == 0 else heads.at[low]).at[rows], heads.at[low, rows],
            head_send.at[0, step, part], head_recv.at[0, step, part], {B: jnp.minimum(b + 1, 7)},
        )
        down = remote(
            (head_ref if step == 0 else heads.at[high]).at[rows], heads.at[high, rows],
            head_send.at[1, step, part], head_recv.at[1, step, part], {B: jnp.maximum(b - 1, 0)},
        )
        return (
            (up, jnp.logical_and(b < 7, b >= step), b >= step + 1),
            (down, jnp.logical_and(b > 0, b + step <= 7), b + step <= 6),
        )

    def head_start(step, part):
        for copy, sends, _ in head_copies(step, part):
            pl.when(sends)(copy.start)

    def head_arrive(step, part):
        for copy, _, receives in head_copies(step, part):
            pl.when(receives)(copy.wait_recv)

    def head_sent(step, part):
        for copy, sends, _ in head_copies(step, part):
            pl.when(sends)(copy.wait_send)

    def head_next(step):
        for part in range(2):
            head_arrive(step - 1, part)
            head_start(step, part)

    slot = lax.rem(b, 4)
    gives = (b // 4) == c
    part_rows = pl.ds(pl.multiple_of(16 * (2 * y + h), 16), 16)

    def slice_part(at):
        return normed.at[part_rows, pl.ds(pl.multiple_of(512 * at + 128 * x, 128), 128)]

    def slice_at(number):
        return slices.at[y, h, x, c, :, pl.ds(pl.multiple_of(128 * number, 128), 128)]

    slice_copies = [
        remote(slice_part(peer[B]), slice_at(slot), piece_send.at[n], piece_recv.at[slot], peer)
        for n, peer in enumerate(along)
    ]
    own_slice = pltpu.make_async_copy(slice_part(b), slice_at(slot), local_sem.at[2])

    def slices_start():
        @pl.when(gives)
        def _():
            own_slice.start()
            for copy in slice_copies:
                copy.start()

    def slices_arrive():
        for number in range(4):
            arriving = remote(slice_at(number), slice_at(number), piece_send.at[0], piece_recv.at[number], along[0])
            pl.when(b != 4 * c + number)(arriving.wait_recv)
        pl.when(gives)(own_slice.wait)

    def norm_student(n, carry):
        rows = pl.ds(pl.multiple_of(16 * n, 16), 16)
        unit, inv_scale = unit_rows(hidden_ref[rows, :], gain_ref[...])
        normed[rows, :] = unit
        inv_cols[rows, :] = jnp.broadcast_to(inv_scale, (16, 128))
        return carry

    def term_copy(row, layer):
        to = 2 * row + layer
        return to, remote(terms.at[to], got_terms.at[b], term_send.at[to], term_recv.at[b], {B: to})

    def teach(row, layer):
        to, copy = term_copy(row, layer)

        def add_columns(k, total):
            columns = pl.ds(pl.multiple_of(1024 * k, 1024), 1024)
            return total + lax.dot_general(
                head_cols[:, columns], states[row, layer, :, :, :, columns].reshape(128, 1024),
                (((1,), (1,)), ((), ())), preferred_element_type=jnp.float32,
            )

        logits = lax.fori_loop(0, 4, add_columns, jnp.zeros((320, 128), jnp.float32))
        top = jnp.max(logits, axis=0, keepdims=True)
        scaled = jnp.exp(logits - top)
        near_stats[0, 0, pl.ds(to, 1), :] = top
        near_stats[0, 1, pl.ds(to, 1), :] = jnp.sum(scaled, axis=0, keepdims=True)
        terms[to] = scaled.astype(jnp.bfloat16)
        pl.when(to != b)(copy.start)

        @pl.when(to == b)
        def _():
            got_terms[b] = terms[to]

    def joined(stats, count):
        top = stats[0, 0]
        for n in range(1, count):
            top = jnp.maximum(top, stats[n, 0])
        total = jnp.zeros_like(top)
        for n in range(count):
            total += stats[n, 1] * jnp.exp(stats[n, 0] - top)
        return top, total

    def to_all(peers, stats, send, recv):
        for n, peer in enumerate(peers):
            move(stats.at[0], stats.at[n + 1], send.at[n], recv.at[n], peer)

    def from_all(peers, stats, send, recv):
        for n, peer in enumerate(peers):
            arrive(stats.at[n + 1], send.at[n], recv.at[n], peer)

    def near_to_far(close, far, send, recv, far_send, far_recv):
        from_all(near, close, send, recv)
        top, total = joined(close, 4)
        far[0, 0] = top
        far[0, 1] = total
        to_all(there, far, far_send, far_recv)

    def ratio_of(close, far, far_send, far_recv):
        from_all(there, far, far_send, far_recv)
        top, total = joined(far, 16)
        return jnp.exp(close[0, 0] - top) / total

    first_shared, late_shared, thin_shared = [], [], []
    first = [route(states, side, h, first_shared) for side in range(2)]
    late = [route(states, side, 1 - h, late_shared) for side in range(2)]
    thin = [route(slices, side, h, thin_shared) for side in range(2)]
    thin_late = [route(slices, side, 1 - h, thin_shared) for side in range(2)]

    def go(*groups):
        for group in groups:
            for r in group:
                next(r, None)

    across = step_of(states.at[y, h, x, c], {H: 1 - h}, states.at[y, 1 - h, x, c])
    go(first)
    lax.fori_loop(0, 8, norm_student, 0)
    slices_start()
    for part in range(2):
        head_start(0, part)
    go(first)
    slices_arrive()
    thin_across = step_of(slices.at[y, h, x, c], {H: 1 - h}, slices.at[y, 1 - h, x, c])
    go(first, thin)
    head_next(1)
    go(first, thin)
    across()
    go(late, first, thin)
    head_next(2)
    own_teacher_head.wait()
    for wait in first_shared:
        wait()
    go(late)
    teach(0, h)
    teach(1, h)
    go(late)
    teach(2, h)
    teach(3, h)
    thin_across()
    go(late, thin, thin_late)
    head_next(3)
    go(late, thin, thin_late)
    for wait in late_shared:
        wait()
    for row in range(4):
        teach(row, 1 - h)
    to_all(near, near_stats, near_send, near_recv)
    go(thin_late)
    head_next(4)
    near_to_far(near_stats, far_stats, near_send, near_recv, far_send, far_recv)
    go(thin_late)
    head_next(5)
    factor[...] = ratio_of(near_stats, far_stats, far_send, far_recv) * weight_ref[...]
    got_factor[b] = factor[...]
    spread(lambda at: factor, got_factor, factor_send, factor_recv)
    go(thin_late)
    head_next(6)
    for part in range(2):
        head_arrive(6, part)
    own_head.wait()

    def add_block(q, total):
        columns = normed[:, pl.ds(pl.multiple_of(q * 512, 512), 512)]
        return total + lax.dot_general(
            heads[q], columns, (((1,), (1,)), ((), ())), preferred_element_type=jnp.float32
        )

    logits = lax.fori_loop(0, 8, add_block, jnp.zeros((320, 128), jnp.float32))
    local_top = jnp.max(logits, axis=0, keepdims=True)
    scaled = jnp.exp(logits - local_top)
    near_student[0, 0] = jnp.broadcast_to(local_top, (8, 128))
    near_student[0, 1] = jnp.broadcast_to(jnp.sum(scaled, axis=0, keepdims=True), (8, 128))
    to_all(near, near_student, student_near_send, student_near_recv)
    near_to_far(near_student, far_student, student_near_send, student_near_recv, student_far_send, student_far_recv)
    for wait in thin_shared:
        wait()
    for at in range(8):
        for n in range(4):
            joined_slices[at, :, 128 * n : 128 * n + 128] = slices[
                :, :, n, at // 4, :, 128 * (at % 4) : 128 * (at % 4) + 128
            ].reshape(128, 128)
    own_ratio = ratio_of(near_student, far_student, student_far_send, student_far_recv)[0:1]
    collect(got_factor, factor_send, factor_recv)
    for n in range(8):
        waits = remote(got_terms.at[n], got_terms.at[n], term_send.at[n], term_recv.at[n], along[0])
        pl.when(b != n)(waits.wait_recv)

    def add_branch(n, mixed):
        return mixed + got_terms[n].astype(jnp.float32) * got_factor[n, pl.ds(b, 1), :]

    mixed = lax.fori_loop(0, 8, add_branch, jnp.zeros((320, 128), jnp.float32))
    targets = (1.0 - mix_label) * mixed + mix_label * label_ref[...]
    all_grads[b] = (loss_scale * (scaled * own_ratio - targets)).astype(jnp.bfloat16)

    low = 4 * (b // 4)
    mates = [low + ring(slot, step, 4) for step in range(1, 4)]
    sources = [low + ring(slot, -step, 4) for step in range(1, 4)]
    partner = ring(b, 4, 8)
    move(all_grads.at[b], all_grads.at[b], grad_send.at[3], grad_recv.at[3], {B: partner})
    for n, mate in enumerate(mates):
        move(all_grads.at[b], all_grads.at[b], grad_send.at[n], grad_recv.at[n], {B: mate})

    def part(q):
        result = lax.dot_general(
            all_grads[b], heads[q], (((0,), (0,)), ((), ())), preferred_element_type=jnp.float32
        )
        columns = pl.ds(pl.multiple_of(q * 512, 512), 512)
        weighted = hidden_ref[:, columns].astype(jnp.float32) * gain_ref[:, columns]
        return result, jnp.sum(result * weighted, axis=1, keepdims=True)

    column_dots = jnp.zeros((128, 1), jnp.float32)
    for n in range(4):
        result, dot = part(2 * n + (1 - c))
        give_part[n] = result
        column_dots += dot
        move(give_part.at[n], got_part.at[n], part_send.at[n], part_recv.at[n], {C: 1 - c})
    for n in range(4):
        result, dot = part(2 * n + c)
        own_part[n] = result
        column_dots += dot
    dots[0] = jnp.broadcast_to(column_dots, (128, 128)).T[0:8]
    for n, peer in enumerate(there):
        move(dots.at[0], dots_far.at[n], dots_send.at[n], dots_recv.at[n], peer)
    for n in range(4):
        arrive(got_part.at[n], part_send.at[n], part_recv.at[n], {C: 1 - c})
        both = own_part[n] + got_part[n]
        for m in range(4):
            plane_give[n, m] = both[:, 128 * m : 128 * m + 128].astype(jnp.bfloat16)
    for n, peer in enumerate(there):
        move(plane_give.at[peer[Y], peer[X]], plane_got.at[n], plane_send.at[n], plane_recv.at[n], peer)

    def pass_on():
        arrive(all_grads.at[partner], grad_send.at[3], grad_recv.at[3], {B: partner})
        for n, mate in enumerate(mates):
            move(all_grads.at[partner], all_grads.at[partner], grad_send.at[4 + n], grad_recv.at[4 + n], {B: mate})

    def add_head(at):
        grad_head_ref[...] += jnp.dot(all_grads[at], joined_slices[at], preferred_element_type=jnp.float32)

    row_dots = dots[0]
    for n, peer in enumerate(there):
        arrive(dots_far.at[n], dots_send.at[n], dots_recv.at[n], peer)
        row_dots += dots_far[n]
    dots_near[0] = row_dots
    to_all(near, dots_near, dot_near_send, dot_near_recv)
    pass_on()
    block = plane_give[y, x].astype(jnp.float32)
    for n, peer in enumerate(there):
        arrive(plane_got.at[n], plane_send.at[n], plane_recv.at[n], peer)
        block += plane_got[n].astype(jnp.float32)
    turned = block.T
    piece[0] = turned[0:64]
    piece[1] = turned[64:128]
    half_copies = [
        remote(piece.at[core], halves.at[h], half_send.at[core], half_recv.at[h], {H: c, C: core}) for core in range(2)
    ]
    for core, copy in enumerate(half_copies):
        mine = jnp.logical_and(h == c, c == core)
        pl.when(jnp.logical_not(mine))(copy.start)

        @pl.when(mine)
        def _():
            halves[h] = piece[core]

    grad_head_ref[...] = jnp.dot(all_grads[b], joined_slices[b], preferred_element_type=jnp.float32)
    add_head(partner)
    from_all(near, dots_near, dot_near_send, dot_near_recv)
    row_dot = (dots_near[0] + dots_near[1] + dots_near[2] + dots_near[3])[0:1]
    for source in range(2):
        waits = remote(
            halves.at[source], halves.at[source], half_send.at[0], half_recv.at[source], {C: 1 - c}
        )
        pl.when(jnp.logical_not(jnp.logical_and(h == source, c == h)))(waits.wait_recv)
    normed_grads = halves[0] + halves[1]
    inv_scale = inv_cols[...].T[0:1]
    values = cols_ref[...]
    summands = normed_grads * values * inv_scale
    sums[...] = jnp.broadcast_to(
        jnp.sum(jnp.concatenate([summands, summands], axis=0).T, axis=0, keepdims=True), (8, 128)
    )
    got_sums[b] = sums[...]
    spread(lambda at: sums, got_sums, sum_send, sum_recv)
    hidden_out_ref[...] = (
        inv_scale * cols_gain_ref[...] * normed_grads - values * inv_scale**3 * row_dot / width_of_model
    )
    for n, source in enumerate(sources):
        arrive(all_grads.at[source], grad_send.at[n], grad_recv.at[n], {B: partner})
        add_head(source)
    for n, source in enumerate(sources):
        other = ring(source, 4, 8)
        arrive(all_grads.at[other], grad_send.at[4 + n], grad_recv.at[4 + n], {B: partner})
        add_head(other)
    collect(got_sums, sum_send, sum_recv)
    gain = got_sums[0]
    for n in range(1, 8):
        gain += got_sums[n]
    gain_out_ref[...] = gain

    for copy in sent:
        copy.wait_send()
    for step in range(7):
        for part_number in range(2):
            head_sent(step, part_number)

    @pl.when(gives)
    def _():
        for copy in slice_copies:
            copy.wait_send()

    for n in range(8):
        _, copy = term_copy(n // 2, n % 2)
        pl.when(b != n)(copy.wait_send)
    for core, copy in enumerate(half_copies):
        pl.when(jnp.logical_not(jnp.logical_and(h == c, c == core)))(copy.wait_send)


def run(*operands):
    inside = pl.BlockSpec(memory_space=pltpu.VMEM)
    anywhere = pl.BlockSpec(memory_space=pl.ANY)
    f32, bf16 = jnp.float32, jnp.bfloat16
    dma = pltpu.SemaphoreType.DMA
    arrays = [
        ((4, 2, 4, 2, 16, 4096), bf16), ((320, 4096), bf16), ((8, 320, 512), bf16), ((128, 4096), bf16),
        ((4, 2, 4, 2, 16, 512), bf16), ((8, 128, 512), bf16), ((128, 128), f32),
        ((8, 320, 128), bf16), ((8, 320, 128), bf16), ((4, 2, 8, 128), f32), ((16, 2, 8, 128), f32),
        ((4, 2, 8, 128), f32), ((16, 2, 8, 128), f32), ((8, 128), f32), ((8, 8, 128), f32), ((8, 320, 128), bf16),
        ((4, 128, 512), f32), ((4, 128, 512), f32), ((4, 128, 512), f32), ((4, 4, 128, 128), bf16),
        ((15, 128, 128), bf16), ((1, 8, 128), f32), ((4, 8, 128), f32), ((15, 8, 128), f32),
        ((2, 64, 128), f32), ((2, 64, 128), f32), ((8, 128), f32), ((8, 8, 128), f32),
    ]
    counts = [(128,), (2, 7, 2), None, (8,), (3,), (15,), (3,), (15,), (7,), (7,), (4,), (15,), (15,), (3,), (2,), (7,)]
    semaphores = [dma((3,))]
    for count in counts:
        semaphores += [dma((7,)), dma((4,))] if count is None else [dma(count), dma(count)]
    return pl.pallas_call(
        kernel,
        out_shape=(
            jax.ShapeDtypeStruct((320, 512), f32),
            jax.ShapeDtypeStruct((64, 128), f32),
            jax.ShapeDtypeStruct((8, 128), f32),
        ),
        in_specs=[inside, inside, anywhere, inside, inside, anywhere, inside, inside, inside, inside],
        out_specs=(inside,) * 3,
        scratch_shapes=[pltpu.VMEM(*array) for array in arrays] + semaphores,
        compiler_params=pltpu.CompilerParams(collective_id=0, has_side_effects=True, vmem_limit_bytes=56 << 20),
        name="distill",
    )(*operands)


def per_device(
    teacher_hidden, teacher_gain, teacher_head, student_hidden, student_gain, student_head, cluster_weights, token_ids
):
    cols = student_head.shape[1]
    place = lax.axis_index(TOK)
    weight = (cluster_weights[:, 0].astype(jnp.float32) / DEN).reshape(8, 128)
    offset = place * cols
    label = (token_ids[None, :] == offset + jnp.arange(cols, dtype=jnp.int32)[:, None]).astype(jnp.float32)
    hidden_cols = lax.dynamic_slice_in_dim(student_hidden, place * 64, 64, 1).astype(jnp.float32).T
    gain_cols = lax.dynamic_slice_in_dim(student_gain, place * 64, 64, 0)
    grad_head, grad_hidden, grad_gain = run(
        teacher_hidden[0], teacher_gain, teacher_head[0].T, student_hidden, student_gain[None, :], student_head.T,
        weight, label, hidden_cols, jnp.broadcast_to(gain_cols[:, None], (64, 128)),
    )
    return (grad_head.T, grad_hidden.T, grad_gain[0, :64])


def solution(mesh):
    split = Mesh(mesh.devices.reshape(mesh.shape["branch"], 4, 2, 4, 2), (B, *TOK))
    in_specs = (
        P("branch", TOK, None), P("branch", None), P("branch", None, TOK), P("branch", None), P(),
        P("branch", TOK), P(None, "branch"), P("branch"),
    )
    out_specs = (P("branch", TOK), P("branch", TOK), P(TOK))
    return jax.shard_map(per_device, mesh=split, in_specs=in_specs, out_specs=out_specs, check_vma=False)
```

time: 603 us -> 172 us (0.29)
  waiting for transfers between devices: 381 us -> 0 us
  Pallas kernels: 0 us -> 161 us
  blocking collectives: 81.7 us -> 0 us
  starting transfers between devices: 66.6 us -> 0 us
  local copies, waits for them, and re-layouts: 26.8 us -> 6.88 us
  other arithmetic: 21.5 us -> 3.35 us
  between operations: 14.4 us -> 0.66 us
  matrix products: 9.89 us -> 0 us
    all_gather x1 -> x0, waiting for transfers between devices: 211 us -> none  [per_device(): lax.all_gather(teacher_hidden[0], TOK, axis=0, tiled=True)]
    all_to_all x7 -> x0, waiting for transfers between devices: 170 us -> none  [the longest x5 72.7 us: copy_for_each(): return lax.all_to_all(copies, axis, split_axis=0, concat_axis=0, tiled=True)]
    pallas_call x0 -> x1, Pallas kernels: none -> 161 us  [run(): pl.pallas_call(kernel, out_shape=(jax.ShapeDtypeStruct((320, 512), f32),...]
    all_to_all x3 -> x0, blocking collectives: 81.7 us -> none  [the longest x1 51.6 us: summed_rows(): lax.all_to_all(nearer, far, split_axis=0, concat_axis=0, tiled=True)]
    all_to_all x7 -> x0, starting transfers between devices: 66.6 us -> none  [the longest x5 48.7 us: copy_for_each(): return lax.all_to_all(copies, axis, split_axis=0, concat_axis=0, tiled=True)]
    reduce_sum x10 -> x0, other arithmetic: 14.3 us -> none  [the longest x2 7 us: normalize(): jnp.mean(values * values, axis=-1, keepdims=True) + eps]
    dot_general x4 -> x0, matrix products: 9.89 us -> none  [the longest x1 3.27 us: per_device(): jnp.dot(normed, branch_head, preferred_element_type=jnp.float32)]
    all_to_all x2 -> x0, local copies, waits for them, and re-layouts: 6.95 us -> none  [the longest x1 4.7 us: copy_for_each(): return lax.all_to_all(copies, axis, split_axis=0, concat_axis=0, tiled=True)]
  transfers between devices with their start and end apart: 8 -> 0, of which waited for: 7 -> 0; matrix products, arithmetic and copies ran while one was open for 8% -> 0% of each run, Pallas kernels for 0% -> 0%
where the time goes in v3:
time: 172 us
  Pallas kernels  161 us (94%)
  local copies, waits for them, and re-layouts  6.88 us (4%)
  other arithmetic  3.35 us (2%)
    pallas_call x1, Pallas kernels, run(): pl.pallas_call(kernel, out_shape=(jax.ShapeDtypeStruct((320, 512), f32),...  161 us

profile of v3, /device:TPU:1, one launch (start us, length us, event | category | flops | bytes accessed | tf_op | source)
XLA Modules:
  0.0 172.0 jit_solution(10589061016618186037)
XLA Ops:
  0.6 0.8 dynamic_slice.7
  1.4 1.3 convert_multiply_fusion
  2.7 0.8 constant_dynamic-slice_fusion
  3.5 0.1 copy.12
  3.6 0.6 convert_bitcast_fusion.cols_ref
  4.3 0.7 broadcast_in_dim.5.cols_gain_ref
  4.9 1.4 compare_convert_fusion.label_ref
  6.4 161.1 %distill.1 = (f32[320,512]{1,0:T(8,128)}, f32[64,128]{1,0:T(8,128)}, f32[8,128]{1,0:T(8,128)}) custom-call(bf16[16,4096]{1,0:T(8,128)(2,1)} %bitcast.16, f32[1,4096]{1,0:T(1,128)} %teacher_gain_ref.1, bf16[320,4096]{1,0:T(8,128)(2,1)} %bitcast.13, bf16[128,4096]{1,0:T(8,128)(2,1)} %hidden_ref.1, f32[1,4096]{1,0:T(1,128)} %bitcast.18, ...), custom_call_target="tpu_custom_call" | custom-call | tf_op jit(solution)/shard_map/distill/pallas_call | solution.py:491
  167.5 1.2 slice_bitcast_fusion
  168.7 2.0 %copy.15 = f32[512,320]{0,1:T(8,128)} copy(f32[512,320]{0,1:T(8,128)} %bitcast.14) | data formatting | bytes 1310720
  170.7 1.4 copy.16
  (1 shorter events, 0.0 us)

commit v4 on v3

--- a/solution.py
+++ b/solution.py
@@ -22,11 +22,11 @@
 
 def kernel(
     hidden_block_ref, teacher_gain_ref, teacher_head_ref, hidden_ref, gain_ref, head_ref,
-    weight_ref, label_ref, cols_ref, cols_gain_ref,
+    weight_ref, label_ref,
     grad_head_ref, hidden_out_ref, gain_out_ref,
     states, head_cols, heads, normed, slices, joined_slices, inv_cols,
     terms, got_terms, near_stats, far_stats, near_student, far_student, factor, got_factor, all_grads,
-    own_part, give_part, got_part, plane_give, plane_got, dots, dots_near, dots_far, piece, halves, sums, got_sums,
+    own_part, give_part, got_part, plane_give, plane_got, dots, dots_near, dots_far, piece, halves, sums, got_sums, chip,
     local_sem, send_sem, recv_sem, head_send, head_recv, piece_send, piece_recv,
     term_send, term_recv, near_send, near_recv, far_send, far_recv,
     student_near_send, student_near_recv, student_far_send, student_far_recv, factor_send, factor_recv,
@@ -41,7 +41,11 @@
     there = [{Y: ring(y, dy, 4), X: ring(x, dx, 4)} for dy, dx in plane]
 
     barrier = pltpu.get_barrier_semaphore()
-    for peer in near + along + there:
+    column = [
+        {B: ring(b, step, 8), H: ring(h, dh, 2), C: ring(c, dc, 2)}
+        for step in range(8) for dh in range(2) for dc in range(2) if step or dh or dc
+    ]
+    for peer in column + there:
         pl.semaphore_signal(barrier, inc=1, device_id=peer, device_id_type=MESH)
     own_teacher_head = pltpu.make_async_copy(teacher_head_ref, head_cols, local_sem.at[0])
     own_teacher_head.start()
@@ -54,7 +58,7 @@
         return (values * inv_scale * gain).astype(jnp.bfloat16), inv_scale
 
     states[y, h, x, c] = unit_rows(hidden_block_ref[...], teacher_gain_ref[...])[0]
-    pl.semaphore_wait(barrier, len(near) + len(along) + len(there))
+    pl.semaphore_wait(barrier, len(column) + len(there))
 
     numbers = iter(range(128))
     sent = []
@@ -269,48 +273,45 @@
                 next(r, None)
 
     across = step_of(states.at[y, h, x, c], {H: 1 - h}, states.at[y, 1 - h, x, c])
+    for part in range(2):
+        head_start(0, part)
     go(first)
     lax.fori_loop(0, 8, norm_student, 0)
     slices_start()
-    for part in range(2):
-        head_start(0, part)
     go(first)
+    go(first)
+    head_next(1)
     slices_arrive()
     thin_across = step_of(slices.at[y, h, x, c], {H: 1 - h}, slices.at[y, 1 - h, x, c])
     go(first, thin)
-    head_next(1)
-    go(first, thin)
     across()
-    go(late, first, thin)
+    go(late, first)
     head_next(2)
+    go(late, thin)
     own_teacher_head.wait()
     for wait in first_shared:
         wait()
-    go(late)
     teach(0, h)
     teach(1, h)
     go(late)
+    head_next(3)
     teach(2, h)
     teach(3, h)
+    go(late, thin)
     thin_across()
-    go(late, thin, thin_late)
-    head_next(3)
-    go(late, thin, thin_late)
+    go(thin_late)
+    head_next(4)
+    go(late, thin)
     for wait in late_shared:
         wait()
+    head_next(5)
     for row in range(4):
         teach(row, 1 - h)
     to_all(near, near_stats, near_send, near_recv)
-    go(thin_late)
-    head_next(4)
+    go(thin, thin_late)
+    head_next(6)
     near_to_far(near_stats, far_stats, near_send, near_recv, far_send, far_recv)
     go(thin_late)
-    head_next(5)
-    factor[...] = ratio_of(near_stats, far_stats, far_send, far_recv) * weight_ref[...]
-    got_factor[b] = factor[...]
-    spread(lambda at: factor, got_factor, factor_send, factor_recv)
-    go(thin_late)
-    head_next(6)
     for part in range(2):
         head_arrive(6, part)
     own_head.wait()
@@ -327,7 +328,14 @@
     near_student[0, 0] = jnp.broadcast_to(local_top, (8, 128))
     near_student[0, 1] = jnp.broadcast_to(jnp.sum(scaled, axis=0, keepdims=True), (8, 128))
     to_all(near, near_student, student_near_send, student_near_recv)
+    factor[...] = ratio_of(near_stats, far_stats, far_send, far_recv) * (
+        weight_ref[...].astype(jnp.float32) / DEN
+    )
+    got_factor[b] = factor[...]
+    spread(lambda at: factor, got_factor, factor_send, factor_recv)
+    go(thin_late)
     near_to_far(near_student, far_student, student_near_send, student_near_recv, student_far_send, student_far_recv)
+    go(thin_late)
     for wait in thin_shared:
         wait()
     for at in range(8):
@@ -345,7 +353,10 @@
         return mixed + got_terms[n].astype(jnp.float32) * got_factor[n, pl.ds(b, 1), :]
 
     mixed = lax.fori_loop(0, 8, add_branch, jnp.zeros((320, 128), jnp.float32))
-    targets = (1.0 - mix_label) * mixed + mix_label * label_ref[...]
+    place = ((2 * y + h) * 4 + x) * 2 + c
+    entries = lax.broadcasted_iota(jnp.int32, (320, 128), 0) + 320 * place
+    onehot = (entries == label_ref[...]).astype(jnp.float32)
+    targets = (1.0 - mix_label) * mixed + mix_label * onehot
     all_grads[b] = (loss_scale * (scaled * own_ratio - targets)).astype(jnp.bfloat16)
 
     low = 4 * (b // 4)
@@ -377,13 +388,15 @@
     dots[0] = jnp.broadcast_to(column_dots, (128, 128)).T[0:8]
     for n, peer in enumerate(there):
         move(dots.at[0], dots_far.at[n], dots_send.at[n], dots_recv.at[n], peer)
-    for n in range(4):
-        arrive(got_part.at[n], part_send.at[n], part_recv.at[n], {C: 1 - c})
-        both = own_part[n] + got_part[n]
+    for dy in range(4):
+        row = ring(y, dy, 4)
+        arrive(got_part.at[row], part_send.at[row], part_recv.at[row], {C: 1 - c})
+        both = own_part[row] + got_part[row]
         for m in range(4):
-            plane_give[n, m] = both[:, 128 * m : 128 * m + 128].astype(jnp.bfloat16)
-    for n, peer in enumerate(there):
-        move(plane_give.at[peer[Y], peer[X]], plane_got.at[n], plane_send.at[n], plane_recv.at[n], peer)
+            plane_give[row, m] = both[:, 128 * m : 128 * m + 128].astype(jnp.bfloat16)
+        for n, peer in enumerate(there):
+            if plane[n][0] == dy:
+                move(plane_give.at[row, peer[X]], plane_got.at[n], plane_send.at[n], plane_recv.at[n], peer)
 
     def pass_on():
         arrive(all_grads.at[partner], grad_send.at[3], grad_recv.at[3], {B: partner})
@@ -404,6 +417,10 @@
     for n, peer in enumerate(there):
         arrive(plane_got.at[n], plane_send.at[n], plane_recv.at[n], peer)
         block += plane_got[n].astype(jnp.float32)
+    chip_cols = pl.ds(pl.multiple_of(128 * ((2 * y + c) * 4 + x), 128), 128)
+    summands = block * hidden_ref[:, chip_cols].astype(jnp.float32) * inv_cols[...]
+    sums[...] = jnp.broadcast_to(jnp.sum(summands, axis=0, keepdims=True), (8, 128))
+    own_slot = 2 * b + h
     turned = block.T
     piece[0] = turned[0:64]
     piece[1] = turned[64:128]
@@ -418,6 +435,24 @@
         def _():
             halves[h] = piece[core]
 
+    sum_copies = [
+        (step, core, remote(
+            sums, got_sums.at[own_slot], sum_send.at[step, core], sum_recv.at[own_slot],
+            {B: ring(b, step, 8), H: c, C: core},
+        ))
+        for step in range(8) for core in range(2)
+    ]
+    stays = h == c
+    for step, core, copy in sum_copies:
+        if step:
+            copy.start()
+        else:
+            pl.when(jnp.logical_not(jnp.logical_and(stays, c == core)))(copy.start)
+
+    @pl.when(stays)
+    def _():
+        got_sums[own_slot] = sums[...]
+
     grad_head_ref[...] = jnp.dot(all_grads[b], joined_slices[b], preferred_element_type=jnp.float32)
     add_head(partner)
     from_all(near, dots_near, dot_near_send, dot_near_recv)
@@ -429,15 +464,13 @@
         pl.when(jnp.logical_not(jnp.logical_and(h == source, c == h)))(waits.wait_recv)
     normed_grads = halves[0] + halves[1]
     inv_scale = inv_cols[...].T[0:1]
-    values = cols_ref[...]
-    summands = normed_grads * values * inv_scale
-    sums[...] = jnp.broadcast_to(
-        jnp.sum(jnp.concatenate([summands, summands], axis=0).T, axis=0, keepdims=True), (8, 128)
-    )
-    got_sums[b] = sums[...]
-    spread(lambda at: sums, got_sums, sum_send, sum_recv)
+    own_cols = pl.ds(pl.multiple_of(128 * ((2 * y + h) * 4 + x), 128), 128)
+    chip[0] = hidden_ref[:, own_cols].astype(jnp.float32).T
+    chip[1] = jnp.broadcast_to(gain_ref[:, own_cols], (128, 128)).T
+    own_rows = pl.ds(pl.multiple_of(64 * c, 64), 64)
+    values, gain_cols = chip[0, own_rows, :], chip[1, own_rows, :]
     hidden_out_ref[...] = (
-        inv_scale * cols_gain_ref[...] * normed_grads - values * inv_scale**3 * row_dot / width_of_model
+        inv_scale * gain_cols * normed_grads - values * inv_scale**3 * row_dot / width_of_model
     )
     for n, source in enumerate(sources):
         arrive(all_grads.at[source], grad_send.at[n], grad_recv.at[n], {B: partner})
@@ -446,12 +479,19 @@
         other = ring(source, 4, 8)
         arrive(all_grads.at[other], grad_send.at[4 + n], grad_recv.at[4 + n], {B: partner})
         add_head(other)
-    collect(got_sums, sum_send, sum_recv)
+    for n in range(16):
+        waits = remote(got_sums.at[n], got_sums.at[n], sum_send.at[0, 0], sum_recv.at[n], along[0])
+        pl.when(jnp.logical_not(jnp.logical_and(stays, own_slot == n)))(waits.wait_recv)
     gain = got_sums[0]
-    for n in range(1, 8):
+    for n in range(1, 16):
         gain += got_sums[n]
-    gain_out_ref[...] = gain
-
+    gain_out_ref[...] = jnp.where(c == 0, gain, jnp.concatenate([gain[:, 64:], gain[:, :64]], axis=1))
+
+    for step, core, copy in sum_copies:
+        if step:
+            copy.wait_send()
+        else:
+            pl.when(jnp.logical_not(jnp.logical_and(stays, c == core)))(copy.wait_send)
     for copy in sent:
         copy.wait_send()
     for step in range(7):
@@ -482,12 +522,13 @@
         ((4, 2, 8, 128), f32), ((16, 2, 8, 128), f32), ((8, 128), f32), ((8, 8, 128), f32), ((8, 320, 128), bf16),
         ((4, 128, 512), f32), ((4, 128, 512), f32), ((4, 128, 512), f32), ((4, 4, 128, 128), bf16),
         ((15, 128, 128), bf16), ((1, 8, 128), f32), ((4, 8, 128), f32), ((15, 8, 128), f32),
-        ((2, 64, 128), f32), ((2, 64, 128), f32), ((8, 128), f32), ((8, 8, 128), f32),
+        ((2, 64, 128), f32), ((2, 64, 128), f32), ((8, 128), f32), ((16, 8, 128), f32), ((2, 128, 128), f32),
     ]
-    counts = [(128,), (2, 7, 2), None, (8,), (3,), (15,), (3,), (15,), (7,), (7,), (4,), (15,), (15,), (3,), (2,), (7,)]
+    counts = [(128,), (2, 7, 2), None, (8,), (3,), (15,), (3,), (15,), (7,), (7,), (4,), (15,), (15,), (3,), (2,)]
     semaphores = [dma((3,))]
     for count in counts:
         semaphores += [dma((7,)), dma((4,))] if count is None else [dma(count), dma(count)]
+    semaphores += [dma((8, 2)), dma((16,))]
     return pl.pallas_call(
         kernel,
         out_shape=(
@@ -495,7 +536,7 @@
             jax.ShapeDtypeStruct((64, 128), f32),
             jax.ShapeDtypeStruct((8, 128), f32),
         ),
-        in_specs=[inside, inside, anywhere, inside, inside, anywhere, inside, inside, inside, inside],
+        in_specs=[inside, inside, anywhere, inside, inside, anywhere, inside, inside],
         out_specs=(inside,) * 3,
         scratch_shapes=[pltpu.VMEM(*array) for array in arrays] + semaphores,
         compiler_params=pltpu.CompilerParams(collective_id=0, has_side_effects=True, vmem_limit_bytes=56 << 20),
@@ -506,16 +547,9 @@
 def per_device(
     teacher_hidden, teacher_gain, teacher_head, student_hidden, student_gain, student_head, cluster_weights, token_ids
 ):
-    cols = student_head.shape[1]
-    place = lax.axis_index(TOK)
-    weight = (cluster_weights[:, 0].astype(jnp.float32) / DEN).reshape(8, 128)
-    offset = place * cols
-    label = (token_ids[None, :] == offset + jnp.arange(cols, dtype=jnp.int32)[:, None]).astype(jnp.float32)
-    hidden_cols = lax.dynamic_slice_in_dim(student_hidden, place * 64, 64, 1).astype(jnp.float32).T
-    gain_cols = lax.dynamic_slice_in_dim(student_gain, place * 64, 64, 0)
     grad_head, grad_hidden, grad_gain = run(
         teacher_hidden[0], teacher_gain, teacher_head[0].T, student_hidden, student_gain[None, :], student_head.T,
-        weight, label, hidden_cols, jnp.broadcast_to(gain_cols[:, None], (64, 128)),
+        cluster_weights.reshape(8, 128), token_ids[None, :],
     )
     return (grad_head.T, grad_hidden.T, grad_gain[0, :64])
 

time: 172 us -> 162 us (0.942)
  Pallas kernels: 161 us -> 157 us
  other arithmetic: 3.35 us -> 0 us
  local copies, waits for them, and re-layouts: 6.88 us -> 4.54 us
    pallas_call x1, Pallas kernels: 161 us -> 157 us  [run(): pl.pallas_call(kernel, out_shape=(jax.ShapeDtypeStruct((320, 512), f32),...]
where the time goes in v4:
time: 162 us
  Pallas kernels  157 us (97%)
  local copies, waits for them, and re-layouts  4.54 us (3%)
    pallas_call x1, Pallas kernels, run(): pl.pallas_call(kernel, out_shape=(jax.ShapeDtypeStruct((320, 512), f32),...  157 us
    unnamed x2, local copies, waits for them, and re-layouts  3.34 us

profile of v4, /device:TPU:1, one launch (start us, length us, event | category | flops | bytes accessed | tf_op | source)
XLA Modules:
  0.0 161.7 jit_solution(17007834208331424607)
XLA Ops:
  0.6 156.6 %distill.1 = (f32[320,512]{1,0:T(8,128)}, f32[64,128]{1,0:T(8,128)}, f32[8,128]{1,0:T(8,128)}) custom-call(bf16[16,4096]{1,0:T(8,128)(2,1)} %bitcast.15, f32[1,4096]{1,0:T(1,128)} %teacher_gain_ref.1, bf16[320,4096]{1,0:T(8,128)(2,1)} %bitcast.12, bf16[128,4096]{1,0:T(8,128)(2,1)} %hidden_ref.1, f32[1,4096]{1,0:T(1,128)} %bitcast.17, ...), custom_call_target="tpu_custom_call" | custom-call | tf_op jit(solution)/shard_map/distill/pallas_call | solution.py:532
  157.2 1.2 slice_bitcast_fusion
  158.4 2.0 %copy.13 = f32[512,320]{0,1:T(8,128)} copy(f32[512,320]{0,1:T(8,128)} %bitcast.13) | data formatting | bytes 1310720
  160.4 1.4 copy.14

commit v5 on v4

--- a/solution.py
+++ b/solution.py
@@ -58,6 +58,14 @@
         return (values * inv_scale * gain).astype(jnp.bfloat16), inv_scale
 
     states[y, h, x, c] = unit_rows(hidden_block_ref[...], teacher_gain_ref[...])[0]
+    def norm_student(n, carry):
+        rows = pl.ds(pl.multiple_of(16 * n, 16), 16)
+        unit, inv_scale = unit_rows(hidden_ref[rows, :], gain_ref[...])
+        normed[rows, :] = unit
+        inv_cols[rows, :] = jnp.broadcast_to(inv_scale, (16, 128))
+        return carry
+
+    lax.fori_loop(0, 8, norm_student, 0)
     pl.semaphore_wait(barrier, len(column) + len(there))
 
     numbers = iter(range(128))
@@ -138,7 +146,7 @@
         share(2)
 
     def head_copies(step, part):
-        rows = pl.ds(160 * part, 160)
+        rows = pl.ds(80 * part, 80)
         low, high = jnp.maximum(b - step, 0), jnp.minimum(b + step, 7)
         up = remote(
             (head_ref if step == 0 else heads.at[low]).at[rows], heads.at[low, rows],
@@ -166,7 +174,7 @@
             pl.when(sends)(copy.wait_send)
 
     def head_next(step):
-        for part in range(2):
+        for part in range(4):
             head_arrive(step - 1, part)
             head_start(step, part)
 
@@ -199,19 +207,12 @@
             pl.when(b != 4 * c + number)(arriving.wait_recv)
         pl.when(gives)(own_slice.wait)
 
-    def norm_student(n, carry):
-        rows = pl.ds(pl.multiple_of(16 * n, 16), 16)
-        unit, inv_scale = unit_rows(hidden_ref[rows, :], gain_ref[...])
-        normed[rows, :] = unit
-        inv_cols[rows, :] = jnp.broadcast_to(inv_scale, (16, 128))
-        return carry
-
     def term_copy(row, layer):
         to = 2 * row + layer
         return to, remote(terms.at[to], got_terms.at[b], term_send.at[to], term_recv.at[b], {B: to})
 
     def teach(row, layer):
-        to, copy = term_copy(row, layer)
+        to = 2 * row + layer
 
         def add_columns(k, total):
             columns = pl.ds(pl.multiple_of(1024 * k, 1024), 1024)
@@ -226,11 +227,14 @@
         near_stats[0, 0, pl.ds(to, 1), :] = top
         near_stats[0, 1, pl.ds(to, 1), :] = jnp.sum(scaled, axis=0, keepdims=True)
         terms[to] = scaled.astype(jnp.bfloat16)
-        pl.when(to != b)(copy.start)
-
         @pl.when(to == b)
         def _():
             got_terms[b] = terms[to]
+
+    def terms_start():
+        for number in range(8):
+            _, copy = term_copy(number // 2, number % 2)
+            pl.when(b != number)(copy.start)
 
     def joined(stats, count):
         top = stats[0, 0]
@@ -273,10 +277,9 @@
                 next(r, None)
 
     across = step_of(states.at[y, h, x, c], {H: 1 - h}, states.at[y, 1 - h, x, c])
-    for part in range(2):
+    for part in range(4):
         head_start(0, part)
     go(first)
-    lax.fori_loop(0, 8, norm_student, 0)
     slices_start()
     go(first)
     go(first)
@@ -308,11 +311,12 @@
     for row in range(4):
         teach(row, 1 - h)
     to_all(near, near_stats, near_send, near_recv)
+    terms_start()
     go(thin, thin_late)
     head_next(6)
     near_to_far(near_stats, far_stats, near_send, near_recv, far_send, far_recv)
     go(thin_late)
-    for part in range(2):
+    for part in range(4):
         head_arrive(6, part)
     own_head.wait()
 
@@ -495,7 +499,7 @@
     for copy in sent:
         copy.wait_send()
     for step in range(7):
-        for part_number in range(2):
+        for part_number in range(4):
             head_sent(step, part_number)
 
     @pl.when(gives)
@@ -524,7 +528,7 @@
         ((15, 128, 128), bf16), ((1, 8, 128), f32), ((4, 8, 128), f32), ((15, 8, 128), f32),
         ((2, 64, 128), f32), ((2, 64, 128), f32), ((8, 128), f32), ((16, 8, 128), f32), ((2, 128, 128), f32),
     ]
-    counts = [(128,), (2, 7, 2), None, (8,), (3,), (15,), (3,), (15,), (7,), (7,), (4,), (15,), (15,), (3,), (2,)]
+    counts = [(128,), (2, 7, 4), None, (8,), (3,), (15,), (3,), (15,), (7,), (7,), (4,), (15,), (15,), (3,), (2,)]
     semaphores = [dma((3,))]
     for count in counts:
         semaphores += [dma((7,)), dma((4,))] if count is None else [dma(count), dma(count)]

time: 162 us -> 152 us (0.938)
  Pallas kernels: 157 us -> 146 us
    pallas_call x1, Pallas kernels: 157 us -> 146 us  [run(): pl.pallas_call(kernel, out_shape=(jax.ShapeDtypeStruct((320, 512), f32),...]
where the time goes in v5:
time: 152 us
  Pallas kernels  146 us (96%)
  local copies, waits for them, and re-layouts  4.54 us (3%)
    pallas_call x1, Pallas kernels, run(): pl.pallas_call(kernel, out_shape=(jax.ShapeDtypeStruct((320, 512), f32),...  146 us
    unnamed x2, local copies, waits for them, and re-layouts  3.34 us

profile of v5, /device:TPU:1, one launch (start us, length us, event | category | flops | bytes accessed | tf_op | source)
XLA Modules:
  0.0 151.6 jit_solution(2560488343332800495)
XLA Ops:
  0.6 146.4 %distill.1 = (f32[320,512]{1,0:T(8,128)}, f32[64,128]{1,0:T(8,128)}, f32[8,128]{1,0:T(8,128)}) custom-call(bf16[16,4096]{1,0:T(8,128)(2,1)} %bitcast.15, f32[1,4096]{1,0:T(1,128)} %teacher_gain_ref.1, bf16[320,4096]{1,0:T(8,128)(2,1)} %bitcast.12, bf16[128,4096]{1,0:T(8,128)(2,1)} %hidden_ref.1, f32[1,4096]{1,0:T(1,128)} %bitcast.17, ...), custom_call_target="tpu_custom_call" | custom-call | tf_op jit(solution)/shard_map/distill/pallas_call | solution.py:536
  147.0 1.2 slice_bitcast_fusion
  148.2 2.0 %copy.13 = f32[512,320]{0,1:T(8,128)} copy(f32[512,320]{0,1:T(8,128)} %bitcast.13) | data formatting | bytes 1310720
  150.2 1.4 copy.14
